TPU v7x, 32 devices: a whole 2x2x4 slice. The times are simulated.
32 devices in a mesh: runs: 2 (over x), space: 16 (over z, y, core).
Axes of the slice: x: 2, y: 2, z: 4, core: 2. Of those that a mesh axis runs over, the one named last changes fastest.
Arguments:
- tangent: float32 [1024, 256, 128], P('runs', 'space'), parts along dimension 0, may hold values from -400 to 400
- courant_x: float32 [512, 128], P(('runs', 'space')), parts along dimension 0, may hold values from -0.4 to 0.4
- courant_y: float32 [512, 128], P(('runs', 'space')), parts along dimension 0, may hold values from -0.4 to 0.4
Outputs:
- basis: float32 [1024, 256, 128], P('runs', 'space'), parts along dimension 0
- growth: float32 [1024, 512], P('runs'), parts along dimension 0
- log_growth: float32 [1024], P('runs'), parts along dimension 0
- first_factor: float32 [1024, 512], P('runs'), parts along dimension 0
There are 2 independent parts, one for each index of `runs`. A program takes and returns all parts, laid end to end along the dimension named above; each array names one. Nothing has to cross between parts.
All inputs are finite; a program needn't handle non-finite values.
Results may differ from a plain program's by a relative error of at most 0.0012.
Values sent between devices are 32-bit elements; how exact they have to be, the bound alone decides.
A program may use at most 128 MiB of HBM per device.

v0:
```python
import jax
import jax.numpy as jnp
from jax import lax
from jax.sharding import PartitionSpec as P

diffusion_number = 0.2


def extended(cells, sides, width):
    for axis, dim in sides:
        count = lax.axis_size(axis)
        head = lax.slice_in_dim(cells, 0, width, axis=dim)
        tail = lax.slice_in_dim(cells, cells.shape[dim] - width, cells.shape[dim], axis=dim)
        cells = jnp.concatenate(
            [
                lax.ppermute(tail, axis, [(i, (i + 1) % count) for i in range(count)]),
                cells,
                lax.ppermute(head, axis, [((i + 1) % count, i) for i in range(count)]),
            ],
            axis=dim,
        )
    return cells


def update(center, east_side, west_side, courant_x, courant_y):
    north_side = jnp.roll(center, -1, 2)
    south_side = jnp.roll(center, 1, 2)
    spread = east_side + west_side + north_side + south_side - 4.0 * center
    return (
        center
        + diffusion_number * spread
        - 0.5 * courant_x * (east_side - west_side)
        - 0.5 * courant_y * (north_side - south_side)
    )


def single_step(field, courant_x, courant_y):
    padded = extended(field, (("space", 1),), 1)
    return update(padded[:, 1:-1], padded[:, 2:], padded[:, :-2], courant_x, courant_y)


def factorize(gram, flattened):
    lower = jnp.linalg.cholesky(gram)
    identity = jnp.eye(gram.shape[0], dtype=jnp.float32)
    inverse = lax.linalg.triangular_solve(lower, identity, left_side=True, lower=True)
    return (lower, jnp.dot(inverse, flattened, precision=lax.Precision.HIGHEST))


def body(tangent, courant_x, courant_y):
    advanced = single_step(single_step(tangent, courant_x, courant_y), courant_x, courant_y)
    vectors = advanced.shape[0]
    flattened = advanced.reshape(vectors, advanced.shape[1] * advanced.shape[2])
    cells = advanced.shape[1] * advanced.shape[2] * lax.axis_size("space")
    first_part = jnp.dot(flattened, flattened.T, precision=lax.Precision.HIGHEST)
    first_gram = lax.psum(first_part, "space") / cells
    first_lower, first_basis = factorize(first_gram, flattened)
    second_part = jnp.dot(first_basis, first_basis.T, precision=lax.Precision.HIGHEST)
    second_gram = lax.psum(second_part, "space") / cells
    second_lower, final_basis = factorize(second_gram, first_basis)
    growth = jnp.dot(first_lower, second_lower, precision=lax.Precision.HIGHEST).T
    log_growth = jnp.log(jnp.diagonal(first_lower)) + jnp.log(jnp.diagonal(second_lower))
    return (final_basis.reshape(advanced.shape), growth, log_growth, first_lower.T)


def solution(mesh):
    return jax.shard_map(
        body,
        mesh=mesh,
        in_specs=(P("runs", "space", None), P(("runs", "space"), None), P(("runs", "space"), None)),
        out_specs=(P("runs", "space", None), P("runs", None), P("runs"), P("runs", None)),
        check_vma=False,
    )
```

profile of v0, /device:TPU:0, one launch (start us, length us, event | category | flops | bytes accessed | tf_op | source)
XLA Modules:
  0.0 612.7 jit_solution(12937679501652068149)
XLA Ops:
  7.2 2.6 fusion.97
  9.8 5.5 collective-permute-start
  15.3 5.2 copy.47
  20.5 8.2 %fusion.98 = (f32[512,16,127]{0,2,1:T(8,128)}, f32[512,16,127]{0,2,1:T(8,128)}) fusion(f32[512,16,128]{0,2,1:T(8,128)} %copy.47), kind=kLoop, calls=%fused_computation.177 | loop fusion | bytes 16646144 | tf_op jit(solution)/shard_map/jit(_roll_static)/slice | solution.py:26
  30.1 9.0 %multiply_subtract_fusion.1 = f32[512,16,128]{0,2,1:T(8,128)S(1)} fusion(f32[512,16,128]{0,2,1:T(8,128)} %copy.47, f32[512,16,127]{0,2,1:T(8,128)} %get-tuple-element.71, f32[512,16,1]{0,2,1:T(1,128)S(1)} %get-tuple-element.73, f32[512,16,1]{0,2,1:T(1,128)S(1)} %get-tuple-element.72, f32[512,16,127]{0,2,1:T(8,128)} %get-tuple-element.70, ...), kind=kLoop, calls=%fused_computation.15 | loop fusion | flops 17825792 | bytes 17317888 | tf_op jit(solution)/shard_map/sub | solution.py:30
  39.1 2.0 copy-done.2
  41.3 4.5 collective-permute-start.2
  46.2 8.2 %fusion.95 = (f32[512,16,127]{0,2,1:T(8,128)}, f32[512,16,127]{0,2,1:T(8,128)}) fusion(f32[512,16,128]{0,2,1:T(8,128)} %copy-done.2), kind=kLoop, calls=%fused_computation.174 | loop fusion | bytes 16646144 | tf_op jit(solution)/shard_map/jit(_roll_static)/slice | solution.py:26
  55.8 9.0 %multiply_subtract_fusion = f32[512,16,128]{0,2,1:T(8,128)S(1)} fusion(f32[512,16,128]{0,2,1:T(8,128)} %copy-done.2, f32[512,16,127]{0,2,1:T(8,128)} %get-tuple-element.65, f32[512,16,1]{0,2,1:T(1,128)S(1)} %get-tuple-element.67, f32[512,16,1]{0,2,1:T(1,128)S(1)} %get-tuple-element.66, f32[512,16,127]{0,2,1:T(8,128)} %get-tuple-element.64, ...), kind=kLoop, calls=%fused_computation.14 | loop fusion | flops 17825792 | bytes 17317888 | tf_op jit(solution)/shard_map/sub | solution.py:30
  64.8 2.0 copy-done.3
  66.8 8.0 %convolution_bitcast_fusion.1 = f32[512,512]{0,1:T(8,128)} fusion(f32[512,16,128]{0,2,1:T(8,128)S(1)} %multiply_subtract_fusion), kind=kOutput, calls=%fused_computation.17 | convolution fusion | flops 6442450944 | bytes 5242880 | tf_op jit(solution)/shard_map/dot_general | solution.py:54
  75.2 94.1 %all-reduce.4.cloned.1.call-done = f32[512,512]{0,1:T(8,128)} async-done(((f32[512,512]{0,1:T(8,128)}), f32[512,512]{0,1:T(8,128)}) %all-reduce.4.cloned.1.call-update) | async-done | bytes 1048592 | tf_op jit(solution)/shard_map/psum | solution.py:55
  169.3 2.4 broadcast_multiply_fusion.1
  171.7 1.6 copy.55
  174.5 11.7 %cholesky.286 = f32[128,128]{1,0:T(8,128)S(1)} custom-call(f32[128,128]{1,0:T(8,128)S(1)} %cholesky.426), custom_call_target="Cholesky" | custom-call | tf_op jit(solution)/shard_map/jit(cholesky)/cholesky | solution.py:43
  186.3 9.8 %custom-call.31 = f32[1,128,128]{1,2,0:T(8,128)S(1)} custom-call(f32[1,128,128]{2,1,0:T(8,128)S(1)} %get-tuple-element.93), custom_call_target="InvertDiagBlocksLowerTriangular" | custom-call | tf_op jit(solution)/shard_map/jit(cholesky)/cholesky | solution.py:43
  197.4 1.3 convolution_subtract_fusion.7
  198.7 11.7 %cholesky.305 = f32[128,128]{1,0:T(8,128)S(1)} custom-call(f32[128,128]{1,0:T(8,128)S(1)} %cholesky.430), custom_call_target="Cholesky" | custom-call | tf_op jit(solution)/shard_map/jit(cholesky)/cholesky | solution.py:43
  211.8 10.2 %custom-call.32 = f32[1,128,128]{1,2,0:T(8,128)S(1)} custom-call(f32[1,128,128]{2,1,0:T(8,128)S(1)} %get-tuple-element.90), custom_call_target="InvertDiagBlocksLowerTriangular" | custom-call | tf_op jit(solution)/shard_map/jit(cholesky)/cholesky | solution.py:43
  222.3 1.3 convolution_subtract_fusion.9
  223.6 11.7 %cholesky.326 = f32[128,128]{1,0:T(8,128)S(1)} custom-call(f32[128,128]{1,0:T(8,128)S(1)} %cholesky.435), custom_call_target="Cholesky" | custom-call | tf_op jit(solution)/shard_map/jit(cholesky)/cholesky | solution.py:43
  236.0 9.8 %custom-call.33 = f32[1,128,128]{1,2,0:T(8,128)S(1)} custom-call(f32[1,128,128]{2,1,0:T(8,128)S(1)} %get-tuple-element.87), custom_call_target="InvertDiagBlocksLowerTriangular" | custom-call | tf_op jit(solution)/shard_map/jit(cholesky)/cholesky | solution.py:43
  247.3 11.9 %cholesky.343 = f32[128,128]{1,0:T(8,128)S(1)} custom-call(f32[128,128]{1,0:T(8,128)S(1)} %convolution_subtract_fusion.11), custom_call_target="Cholesky" | custom-call | tf_op jit(solution)/shard_map/jit(cholesky)/cholesky | solution.py:43
  263.6 11.7 %while.4 = (s32[]{:T(128)}, f32[512,512]{1,0:T(8,128)}, s32[4,2]{0,1:T(2,128)S(1)}, f32[4,128,128]{2,1,0:T(8,128)S(1)}, s32[]{:T(128)}) while((s32[]{:T(128)}, f32[512,512]{1,0:T(8,128)}, s32[4,2]{0,1:T(2,128)S(1)}, f32[4,128,128]{2,1,0:T(8,128)S(1)}, s32[]{:T(128)}) %tuple.67), condition=%wide.while_cond, body=%wide.while_body.sunk | while | flops 2 | bytes 131181 | solution.py:45
  264.3 2.2 bitcast_dynamic-update-slice_fusion.4
  267.2 2.2 bitcast_dynamic-update-slice_fusion.4
  270.2 2.2 bitcast_dynamic-update-slice_fusion.4
  273.1 2.2 bitcast_dynamic-update-slice_fusion.4
  275.3 39.3 %custom-call.34 = f32[4,128,128]{1,2,0:T(8,128)S(1)} custom-call(f32[4,128,128]{2,1,0:T(8,128)S(1)} %get-tuple-element.20), custom_call_target="InvertDiagBlocksLowerTriangular" | custom-call | tf_op jit(solution)/shard_map/triangular_solve/custom-call.3 | solution.py:45
  315.1 1.4 convolution_subtract_fusion.3
  317.0 1.3 convolution_subtract_fusion.2
  318.7 1.6 convolution_subtract_fusion.5
  320.7 7.1 %fusion = f32[512,2048]{1,0:T(8,128)S(1)} fusion(f32[512,2048]{0,1:T(8,128)S(1)} %bitcast.116, f32[128,512]{1,0:T(8,128)S(1)} %fusion.64, f32[128,512]{1,0:T(8,128)S(1)} %fusion.65, f32[128,512]{1,0:T(8,128)S(1)} %fusion.67, f32[128,512]{1,0:T(8,128)S(1)} %fusion.42), kind=kOutput, calls=%fused_computation.34 | convolution fusion | flops 6443237376 | bytes 9437184 | tf_op jit(solution)/shard_map/dot_general | solution.py:46
  327.9 2.0 copy-done
  329.9 8.3 %fusion.100 = f32[512,512]{0,1:T(8,128)} fusion(f32[512,2048]{1,0:T(8,128)S(1)} %fusion), kind=kOutput, calls=%fused_computation.179 | convolution fusion | flops 6442450944 | bytes 5242880 | tf_op jit(solution)/shard_map/dot_general | solution.py:57
  338.3 4.5 gather_fusion
  342.8 1.3 copy.58
  344.1 86.8 %all-reduce.6.cloned.1.call-done = f32[512,512]{0,1:T(8,128)} async-done(((f32[512,512]{0,1:T(8,128)}), f32[512,512]{0,1:T(8,128)}) %all-reduce.6.cloned.1.call-update) | async-done | bytes 1048592 | tf_op jit(solution)/shard_map/psum | solution.py:58
  430.9 2.4 broadcast_multiply_fusion
  433.3 2.6 copy.57
  435.9 1.5 fusion.15
  438.3 11.7 %cholesky.358 = f32[128,128]{1,0:T(8,128)S(1)} custom-call(f32[128,128]{1,0:T(8,128)S(1)} %cholesky.439), custom_call_target="Cholesky" | custom-call | tf_op jit(solution)/shard_map/jit(cholesky)/cholesky | solution.py:43
  450.2 9.8 %custom-call.35 = f32[1,128,128]{1,2,0:T(8,128)S(1)} custom-call(f32[1,128,128]{2,1,0:T(8,128)S(1)} %get-tuple-element.83), custom_call_target="InvertDiagBlocksLowerTriangular" | custom-call | tf_op jit(solution)/shard_map/jit(cholesky)/cholesky | solution.py:43
  461.3 1.3 convolution_subtract_fusion.6
  462.6 11.7 %cholesky.377 = f32[128,128]{1,0:T(8,128)S(1)} custom-call(f32[128,128]{1,0:T(8,128)S(1)} %cholesky.443), custom_call_target="Cholesky" | custom-call | tf_op jit(solution)/shard_map/jit(cholesky)/cholesky | solution.py:43
  475.7 10.0 %custom-call.36 = f32[1,128,128]{1,2,0:T(8,128)S(1)} custom-call(f32[1,128,128]{2,1,0:T(8,128)S(1)} %get-tuple-element.80), custom_call_target="InvertDiagBlocksLowerTriangular" | custom-call | tf_op jit(solution)/shard_map/jit(cholesky)/cholesky | solution.py:43
  485.9 1.3 convolution_subtract_fusion.8
  487.2 11.7 %cholesky.398 = f32[128,128]{1,0:T(8,128)S(1)} custom-call(f32[128,128]{1,0:T(8,128)S(1)} %cholesky.448), custom_call_target="Cholesky" | custom-call | tf_op jit(solution)/shard_map/jit(cholesky)/cholesky | solution.py:43
  499.6 9.8 %custom-call.37 = f32[1,128,128]{1,2,0:T(8,128)S(1)} custom-call(f32[1,128,128]{2,1,0:T(8,128)S(1)} %get-tuple-element.77), custom_call_target="InvertDiagBlocksLowerTriangular" | custom-call | tf_op jit(solution)/shard_map/jit(cholesky)/cholesky | solution.py:43
  510.9 11.9 %cholesky.415 = f32[128,128]{1,0:T(8,128)S(1)} custom-call(f32[128,128]{1,0:T(8,128)S(1)} %convolution_subtract_fusion.10), custom_call_target="Cholesky" | custom-call | tf_op jit(solution)/shard_map/jit(cholesky)/cholesky | solution.py:43
  526.1 2.4 fusion.20
  528.5 4.5 gather_fusion.1
  533.0 4.5 fusion.101
  537.6 11.7 %while.5 = (s32[]{:T(128)}, f32[512,512]{1,0:T(8,128)}, s32[4,2]{0,1:T(2,128)S(1)}, f32[4,128,128]{2,1,0:T(8,128)S(1)}, s32[]{:T(128)}) while((s32[]{:T(128)}, f32[512,512]{1,0:T(8,128)}, s32[4,2]{0,1:T(2,128)S(1)}, f32[4,128,128]{2,1,0:T(8,128)S(1)}, s32[]{:T(128)}) %tuple.77), condition=%wide.while_cond.clone, body=%wide.while_body.clone.sunk | while | flops 2 | bytes 131181 | solution.py:45
  538.3 2.3 bitcast_dynamic-update-slice_fusion.5
  541.2 2.3 bitcast_dynamic-update-slice_fusion.5
  544.2 2.3 bitcast_dynamic-update-slice_fusion.5
  547.1 2.2 bitcast_dynamic-update-slice_fusion.5
  549.3 39.6 %custom-call.38 = f32[4,128,128]{1,2,0:T(8,128)S(1)} custom-call(f32[4,128,128]{2,1,0:T(8,128)S(1)} %get-tuple-element.21), custom_call_target="InvertDiagBlocksLowerTriangular" | custom-call | tf_op jit(solution)/shard_map/triangular_solve/custom-call.3 | solution.py:45
  589.3 1.4 convolution_subtract_fusion.1
  591.2 1.3 convolution_subtract_fusion
  592.9 1.6 convolution_subtract_fusion.4
  595.0 7.1 %convolution_bitcast_fusion = f32[64,8,16,128]{3,1,2,0:T(8,128)S(1)} fusion(f32[512,2048]{1,0:T(8,128)S(1)} %copy-done.1, f32[128,512]{1,0:T(8,128)S(1)} %fusion.58, f32[128,512]{1,0:T(8,128)S(1)} %fusion.59, f32[128,512]{1,0:T(8,128)S(1)} %fusion.61, f32[128,512]{1,0:T(8,128)S(1)} %fusion.40), kind=kOutput, calls=%fused_computation.16 | convolution fusion | flops 6443237376 | bytes 9437184 | tf_op jit(solution)/shard_map/dot_general | solution.py:46
  602.1 2.9 copy.66
  (106 shorter events, 28.4 us)
Async XLA Ops:
  7.2 162.1 %all-reduce.4.cloned.1.call-start = ((), (), s32[]{:S(2)}) async-start(), calls=%async_computation | async-start | bytes 2097152 | tf_op jit(solution)/shard_map/psum | solution.py:55
  9.8 20.1 %collective-permute-start = (f32[512,1,128]{2,0,1:T(8,128)S(1)}, f32[512,1,128]{2,0,1:T(8,128)S(1)}, u32[]{:S(2)}, u32[]{:S(2)}) collective-permute-start(f32[512,1,128]{2,0,1:T(8,128)S(1)} %bitcast.120), channel_id=1, source_target_pairs={{1,0},{2,1},{3,2},{4,3},{5,4},{6,5},{7,6},{8,7},{9,8},{10,9},{11,1... | collective-permute-start | bytes 786440 | tf_op jit(solution)/shard_map/ppermute | solution.py:18
  15.3 14.7 %collective-permute-start.1 = (f32[512,1,128]{2,0,1:T(8,128)S(1)}, f32[512,1,128]{2,0,1:T(8,128)S(1)}, u32[]{:S(2)}, u32[]{:S(2)}) collective-permute-start(f32[512,1,128]{2,0,1:T(8,128)S(1)} %bitcast.119), channel_id=1, source_target_pairs={{0,1},{1,2},{2,3},{3,4},{4,5},{5,6},{6,7},{7,8},{8,9},{9,10},{10,1... | collective-permute-start | bytes 786440 | tf_op jit(solution)/shard_map/ppermute | solution.py:16
  20.5 8.2 %copy-start.10 = (f32[16,128]{1,0:T(8,128)S(1)}, f32[16,128]{1,0:T(8,128)}, u32[]{:S(2)}) copy-start(f32[16,128]{1,0:T(8,128)} %param.8) | copy-start | bytes 24580
  20.5 8.2 %copy-start.11 = (f32[16,128]{1,0:T(8,128)S(1)}, f32[16,128]{1,0:T(8,128)}, u32[]{:S(2)}) copy-start(f32[16,128]{1,0:T(8,128)} %param.7) | copy-start | bytes 24580
  39.1 2.0 copy-start.2
  41.3 14.2 %collective-permute-start.2 = (f32[512,1,128]{2,0,1:T(8,128)S(1)}, f32[512,1,128]{2,0,1:T(8,128)S(1)}, u32[]{:S(2)}, u32[]{:S(2)}) collective-permute-start(f32[512,1,128]{2,0,1:T(8,128)S(1)} %copy.48), channel_id=1, source_target_pairs={{1,0},{2,1},{3,2},{4,3},{5,4},{6,5},{7,6},{8,7},{9,8},{10,9},{11,1... | collective-permute-start | bytes 786440 | tf_op jit(solution)/shard_map/ppermute | solution.py:18
  45.9 9.7 %collective-permute-start.3 = (f32[512,1,128]{2,0,1:T(8,128)S(1)}, f32[512,1,128]{2,0,1:T(8,128)S(1)}, u32[]{:S(2)}, u32[]{:S(2)}) collective-permute-start(f32[512,1,128]{2,0,1:T(8,128)S(1)} %copy.50), channel_id=1, source_target_pairs={{0,1},{1,2},{2,3},{3,4},{4,5},{5,6},{6,7},{7,8},{8,9},{9,10},{10,1... | collective-permute-start | bytes 786440 | tf_op jit(solution)/shard_map/ppermute | solution.py:16
  64.7 2.0 copy-start.3
  74.8 356.1 %all-reduce.6.cloned.1.call-start = ((), (), s32[]{:S(2)}) async-start(), calls=%async_computation.1 | async-start | bytes 2097152 | tf_op jit(solution)/shard_map/psum | solution.py:58
  169.3 3.9 copy-start.6
  173.5 1.0 copy-start.8
  314.7 6.1 copy-start.4
  327.9 2.0 copy-start
  430.9 5.0 copy-start.7
  437.4 1.0 copy-start.9
  522.8 3.3 copy-start.5
  588.9 6.1 copy-start.1
Sparse Core Ops, SparseCore 0:
  74.9 94.3 all-reduce.3
  338.4 92.5 all-reduce.5
where the time goes:
time: 618 us; the launch traced here: 613 us
  other arithmetic  267 us (43%)
  waiting for transfers between devices  181 us (29%)
  local copies, waits for them, and re-layouts  76.2 us (12%)
  matrix products  58.1 us (9%)
  between operations  20 us (3%)
  starting transfers between devices  10.5 us (2%)
    another operation x30, other arithmetic, factorize(): lower = jnp.linalg.cholesky(gram)  159 us
    psum x1, waiting for transfers between devices, body(): first_gram = lax.psum(first_part, 'space') / cells  94.1 us
    psum x1, waiting for transfers between devices, body(): second_gram = lax.psum(second_part, 'space') / cells  86.8 us
    another operation x5, other arithmetic, factorize(): lax.linalg.triangular_solve(lower, identity, left_side=True, lower=True)  82.5 us
    another operation x27, local copies, waits for them, and re-layouts, factorize(): lax.linalg.triangular_solve(lower, identity, left_side=True, lower=True)  23.3 us
    slice x4, local copies, waits for them, and re-layouts, update(): north_side = jnp.roll(center, -1, 2)  18.6 us
    sub x2, other arithmetic, update(): center + diffusion_number * spread  17.9 us
    unnamed x27, local copies, waits for them, and re-layouts  17.4 us
  transfers between devices with their start and end apart: 6, of which 2 were waited for; matrix products, arithmetic and copies ran while one was open for 5% of the time, Pallas kernels for 0%

commit v1 on v0

v1 whole, which is shorter than its diff:
```python
import functools

import jax
import jax.numpy as jnp
from jax import lax
from jax.experimental import pallas as pl
from jax.experimental.pallas import tpu as pltpu
from jax.sharding import PartitionSpec as P

diffusion_number = 0.2
T = 128
MICRO = 16
HIGHEST = lax.Precision.HIGHEST
MESH = pl.DeviceIdType.MESH
VMEM_LIMIT = 48 * 1024 * 1024


def dot(a, b, dims):
    return lax.dot_general(a, b, (dims, ((), ())), precision=HIGHEST, preferred_element_type=jnp.float32)


NN = ((1,), (0,))
NT = ((1,), (1,))
TN = ((0,), (0,))


def pair_list(blocks):
    return [(i, j) for i in range(blocks) for j in range(i, blocks)]


def gram_rows(vectors, devices):
    blocks = vectors // T
    rows = blocks * (blocks + 1) // 2 * T
    chunk = -(-rows // (devices * 8)) * 8
    return chunk, chunk * devices


def gram_into(v_ref, packed_ref):
    vectors, width = v_ref.shape
    blocks = vectors // T
    packed_ref[...] = jnp.zeros_like(packed_ref)

    def step(s, _):
        cols = pl.ds(pl.multiple_of(s * 256, 256), 256)
        at = 0
        for i in range(blocks):
            left = v_ref[i * T:(i + 1) * T, cols]
            for j in range(i, blocks):
                packed_ref[at:at + T, :] += dot(left, v_ref[j * T:(j + 1) * T, cols], NT)
                at += T
        return 0

    lax.fori_loop(0, width // 256, step, 0)


def advance_kernel(w_ref, low_ref, high_ref, coef_ref, v_ref, packed_ref):
    vectors = v_ref.shape[0]
    nx = v_ref.shape[1] // T
    kc = 32

    def step(s, _):
        k0 = pl.multiple_of(s * kc, kc)

        def row(e):
            if e < 2:
                return low_ref[pl.ds(e * vectors + k0, kc), :]
            if e >= nx + 2:
                return high_ref[pl.ds((e - nx - 2) * vectors + k0, kc), :]
            return w_ref[pl.ds(k0 * nx + (e - 2), kc, stride=nx), :]

        def apply(west, center, east, e):
            ce, cw, cn, cs = [coef_ref[f, e - 1:e, :] for f in range(4)]
            north = pltpu.roll(center, T - 1, 1)
            south = pltpu.roll(center, 1, 1)
            return ((1.0 - 4.0 * diffusion_number) * center + (ce * east + cw * west)) + (cn * north + cs * south)

        zero = [row(0), row(1)]
        one = []
        for e in range(1, nx + 3):
            zero.append(row(e + 1))
            one.append(apply(zero[-3], zero[-2], zero[-1], e))
            if e >= 3:
                x = e - 3
                v_ref[pl.ds(k0, kc), x * T:(x + 1) * T] = apply(one[-3], one[-2], one[-1], e - 1)
        return 0

    lax.fori_loop(0, vectors // kc, step, 0)
    gram_into(v_ref, packed_ref)


def eliminate(block):
    m = MICRO
    lane = lax.broadcasted_iota(jnp.int32, (m, T), 1)
    sub = lax.broadcasted_iota(jnp.int32, (m, T), 0)
    rows128 = lax.broadcasted_iota(jnp.int32, (T, T), 0)
    lanes128 = lax.broadcasted_iota(jnp.int32, (T, T), 1)
    rest = jnp.concatenate([block, (rows128 == lanes128).astype(jnp.float32)], axis=1)
    uppers, inverses = [], []
    for p in range(T // m):
        panel = rest[:m]
        left = panel[:, :T]
        cols = [jnp.broadcast_to(left[:, p * m + j:p * m + j + 1], (m, T)) for j in range(m)]
        diag = jnp.ones((m, T), jnp.float32)
        for j in range(m):
            d = cols[j][j:j + 1, :]
            mult = jnp.where(sub > j, cols[j] * (1.0 / d), 0.0)
            diag = jnp.where(sub == j, d, diag)
            for k in range(j + 1, m):
                cols[k] = cols[k] - mult * cols[k][j:j + 1, :]
            wide = jnp.concatenate([mult, mult], axis=1)
            panel = panel - wide * panel[j:j + 1, :]
        scale = lax.rsqrt(diag)
        upper = jnp.where(lane >= sub + p * m, panel[:, :T] * scale, 0.0)
        inverse = panel[:, T:] * scale
        uppers.append(upper)
        inverses.append(inverse)
        if p + 1 < T // m:
            product = dot(upper, jnp.concatenate([upper, inverse], axis=1), TN)
            rest = rest[m:] - product[(p + 1) * m:]
    return jnp.concatenate(uppers, axis=0), jnp.concatenate(inverses, axis=0)


def factor_into(packed_ref, cells, z_ref, row_ref, upper_ref, inverse_ref):
    vectors = z_ref.shape[0]
    blocks = vectors // T
    z_ref[...] = jnp.zeros_like(z_ref)
    for at, (i, j) in enumerate(pair_list(blocks)):
        z_ref[i * T:(i + 1) * T, j * T:(j + 1) * T] = packed_ref[at * T:(at + 1) * T, :] / cells
    block_of = lax.broadcasted_iota(jnp.int32, (T, vectors), 1) // T

    def step(b, _):
        here = pl.ds(pl.multiple_of(b * T, T), T)
        upper, inverse = eliminate(z_ref[here, here])
        row_ref[...] = dot(inverse, z_ref[here, :], NN)
        row_ref[:, here] = inverse
        row = row_ref[...]
        upper_ref[here, :] = jnp.where(block_of > b, row, 0.0)
        upper_ref[here, here] = upper
        inverse_ref[here, :] = jnp.where(block_of <= b, row, 0.0)

        def below(c, _):
            there = pl.ds(pl.multiple_of(c * T, T), T)
            old = jnp.where(block_of == b, 0.0, z_ref[there, :])
            z_ref[there, :] = old - dot(row_ref[:, there], row_ref[...], TN)
            return 0

        lax.fori_loop(b + 1, blocks, below, 0)
        return 0

    lax.fori_loop(0, blocks, step, 0)


def first_kernel(cells, packed_ref, v_ref, upper_ref, q_ref, out_ref, z_ref, row_ref, inverse_ref):
    vectors, width = v_ref.shape
    factor_into(packed_ref, cells, z_ref, row_ref, upper_ref, inverse_ref)

    def step(s, _):
        cols = pl.ds(pl.multiple_of(s * 256, 256), 256)
        for i in range(vectors // T):
            q_ref[i * T:(i + 1) * T, cols] = dot(
                inverse_ref[i * T:(i + 1) * T, :(i + 1) * T], v_ref[:(i + 1) * T, cols], NN
            )
        return 0

    lax.fori_loop(0, width // 256, step, 0)
    gram_into(q_ref, out_ref)


def second_kernel(cells, packed_ref, q_ref, first_ref, basis_ref, growth_ref, log_ref, z_ref, row_ref, inverse_ref, upper_ref):
    vectors, width = q_ref.shape
    nx = width // T
    factor_into(packed_ref, cells, z_ref, row_ref, upper_ref, inverse_ref)

    def step(s, _):
        cols = pl.ds(pl.multiple_of(s * 256, 256), 256)
        for i in range(vectors // T):
            value = dot(inverse_ref[i * T:(i + 1) * T, :(i + 1) * T], q_ref[:(i + 1) * T, cols], NN)
            for h in range(2):
                basis_ref[pl.ds(i * T * nx + 2 * s + h, T, stride=nx), :] = value[:, h * T:(h + 1) * T]
        return 0

    lax.fori_loop(0, width // 256, step, 0)
    rows = lax.broadcasted_iota(jnp.int32, (T, T), 0)
    lanes = lax.broadcasted_iota(jnp.int32, (T, T), 1)
    for i in range(vectors // T):
        here = slice(i * T, (i + 1) * T)
        growth_ref[here, :] = dot(upper_ref[here, i * T:], first_ref[i * T:, :], NN)
        one = jnp.sum(jnp.where(rows == lanes, first_ref[here, here], 0.0), axis=0, keepdims=True)
        two = jnp.sum(jnp.where(rows == lanes, upper_ref[here, here], 0.0), axis=0, keepdims=True)
        log_ref[i:i + 1, :] = jnp.log(one) + jnp.log(two)


def reduce_kernel(n, x_ref, o_ref, pair_buf, sum_buf, recv_buf, pair_s, pair_r, rs_s, rs_r, ag_s, ag_r, fw_s, fw_r):
    chips = n // 2
    total = x_ref.shape[0]
    half = total // 2
    chunk = half // chips
    me = lax.axis_index("space")
    chip = me // 2
    core = me % 2
    partner = chip * 2 + (1 - core)

    def peer(k):
        return lax.rem(chip + k, chips) * 2 + core

    def source(k):
        return lax.rem(chip + chips - k, chips)

    barrier = pltpu.get_barrier_semaphore()
    pl.semaphore_signal(barrier, inc=1, device_id={"space": partner}, device_id_type=MESH)

    def greet(k, _):
        pl.semaphore_signal(barrier, inc=1, device_id={"space": peer(k)}, device_id_type=MESH)
        return 0

    lax.fori_loop(1, chips, greet, 0)
    pl.semaphore_wait(barrier, chips)

    mine = pl.multiple_of(core * half, 8)
    other = pl.multiple_of((1 - core) * half, 8)
    swap = pltpu.make_async_remote_copy(
        src_ref=x_ref.at[pl.ds(other, half)], dst_ref=pair_buf, send_sem=pair_s, recv_sem=pair_r,
        device_id={"space": partner}, device_id_type=MESH)
    swap.start()
    swap.wait()
    sum_buf[...] = x_ref[pl.ds(mine, half), :] + pair_buf[...]

    def scatter(k):
        to = lax.rem(chip + k, chips)
        return pltpu.make_async_remote_copy(
            src_ref=sum_buf.at[pl.ds(pl.multiple_of(to * chunk, 8), chunk)], dst_ref=recv_buf.at[k],
            send_sem=rs_s.at[k], recv_sem=rs_r.at[k], device_id={"space": peer(k)}, device_id_type=MESH)

    def start_scatter(k, _):
        scatter(k).start()
        return 0

    lax.fori_loop(1, chips, start_scatter, 0)
    own = pl.ds(pl.multiple_of(chip * chunk, 8), chunk)
    own_out = pl.ds(pl.multiple_of(mine + chip * chunk, 8), chunk)

    def add(k, acc):
        scatter(k).wait_recv()
        return acc + recv_buf[k]

    o_ref[own_out, :] = lax.fori_loop(1, chips, add, sum_buf[own, :])

    def gather(k):
        return pltpu.make_async_remote_copy(
            src_ref=o_ref.at[own_out], dst_ref=o_ref.at[own_out],
            send_sem=ag_s.at[k], recv_sem=ag_r.at[k], device_id={"space": peer(k)}, device_id_type=MESH)

    def forward(k):
        at = pl.ds(pl.multiple_of(mine + source(k) * chunk, 8), chunk)
        return pltpu.make_async_remote_copy(
            src_ref=o_ref.at[at], dst_ref=o_ref.at[at],
            send_sem=fw_s.at[k], recv_sem=fw_r.at[k], device_id={"space": partner}, device_id_type=MESH)

    def start_gather(k, _):
        gather(k).start()
        return 0

    lax.fori_loop(1, chips, start_gather, 0)
    forward(0).start()

    def pass_on(k, _):
        gather(k).wait_recv()
        forward(k).start()
        return 0

    lax.fori_loop(1, chips, pass_on, 0)

    def finish(k, _):
        forward(k).wait()
        return 0

    lax.fori_loop(0, chips, finish, 0)

    def drain(k, _):
        scatter(k).wait_send()
        gather(k).wait_send()
        return 0

    lax.fori_loop(1, chips, drain, 0)


def whole(memory=pltpu.VMEM):
    return pl.BlockSpec(memory_space=memory)


def plain(kernel, outs, ins, scratch=()):
    return pl.pallas_call(
        kernel,
        out_shape=tuple(jax.ShapeDtypeStruct(s, jnp.float32) for s in outs),
        in_specs=[whole()] * ins,
        out_specs=tuple(whole() for _ in outs),
        scratch_shapes=[pltpu.VMEM(s, jnp.float32) for s in scratch],
        compiler_params=pltpu.CompilerParams(vmem_limit_bytes=VMEM_LIMIT),
    )


def all_reduce(packed, n):
    total = packed.shape[0]
    chips = n // 2
    half = total // 2
    sems = pltpu.SemaphoreType.DMA
    return pl.pallas_call(
        functools.partial(reduce_kernel, n),
        out_shape=jax.ShapeDtypeStruct(packed.shape, jnp.float32),
        in_specs=[whole()],
        out_specs=whole(),
        scratch_shapes=[
            pltpu.VMEM((half, T), jnp.float32),
            pltpu.VMEM((half, T), jnp.float32),
            pltpu.VMEM((chips, half // chips, T), jnp.float32),
            sems, sems,
            sems((chips,)), sems((chips,)), sems((chips,)), sems((chips,)), sems((chips,)), sems((chips,)),
        ],
        compiler_params=pltpu.CompilerParams(collective_id=0, has_side_effects=True, vmem_limit_bytes=VMEM_LIMIT),
    )(packed)


def body(tangent, courant_x, courant_y):
    vectors, nx, ny = tangent.shape
    n = lax.axis_size("space")
    width = nx * ny
    cells = float(width * n)

    def edge(a, b):
        rows = jnp.transpose(tangent[:, a:a + 2], (1, 0, 2)).reshape(2 * vectors, ny)
        return jnp.concatenate([rows, courant_x[b:b + 1], courant_y[b:b + 1], jnp.zeros((6, ny), jnp.float32)], axis=0)

    low = lax.ppermute(edge(nx - 2, nx - 1), "space", [(i, (i + 1) % n) for i in range(n)])
    high = lax.ppermute(edge(0, 0), "space", [((i + 1) % n, i) for i in range(n)])
    e = 2 * vectors
    cx = 0.5 * jnp.concatenate([low[e:e + 1], courant_x, high[e:e + 1]], axis=0)
    cy = 0.5 * jnp.concatenate([low[e + 1:e + 2], courant_y, high[e + 1:e + 2]], axis=0)
    coef = jnp.stack([diffusion_number - cx, diffusion_number + cx, diffusion_number - cy, diffusion_number + cy])
    total = gram_rows(vectors, n)[1]
    v, packed = plain(advance_kernel, [(vectors, width), (total, T)], 4)(
        tangent.reshape(vectors * nx, ny), low, high, coef)
    packed = all_reduce(packed, n)
    square = (vectors, vectors)
    row = (T, vectors)
    first_upper, q, packed = plain(
        functools.partial(first_kernel, cells), [square, (vectors, width), (total, T)], 2, [square, row, square],
    )(packed, v)
    packed = all_reduce(packed, n)
    basis, growth, log_growth = plain(
        functools.partial(second_kernel, cells), [(vectors * nx, ny), square, (vectors // T, T)], 3,
        [square, row, square, square],
    )(packed, q, first_upper)
    return basis.reshape(tangent.shape), growth, log_growth.reshape(vectors), first_upper


def solution(mesh):
    return jax.shard_map(
        body,
        mesh=mesh,
        in_specs=(P("runs", "space", None), P(("runs", "space"), None), P(("runs", "space"), None)),
        out_specs=(P("runs", "space", None), P("runs", None), P("runs"), P("runs", None)),
        check_vma=False,
    )
```

time: 618 us -> 167 us (0.27)
  other arithmetic: 267 us -> 0.03 us
  waiting for transfers between devices: 181 us -> 6.77 us
  Pallas kernels: 0 us -> 146 us
  local copies, waits for them, and re-layouts: 76.2 us -> 6.94 us
  matrix products: 58.1 us -> 0 us
  between operations: 20 us -> 0.75 us
    another operation x35 -> x1, other arithmetic: 242 us -> 0.01 us  [body(): jnp.stack([diffusion_number - cx, diffusion_number + cx, diffusion_number...]
    psum x2 -> x0, waiting for transfers between devices: 181 us -> none  [the longest x1 94.1 us: body(): first_gram = lax.psum(first_part, 'space') / cells]
    pallas_call x0 -> x5, Pallas kernels: none -> 146 us  [the longest x2 49 us: all_reduce(): pl.pallas_call(functools.partial(reduce_kernel, n), out_shape=jax.ShapeDt...]
    dot_general x5 -> x0, matrix products: 35.2 us -> none  [the longest x2 14.3 us: factorize(): return (lower, jnp.dot(inverse, flattened, precision=lax.Precision.HIGHEST))]
    another operation x35 -> x1, local copies, waits for them, and re-layouts: 23.6 us -> 0.01 us  [the longest x27 23.3 us: factorize(): lax.linalg.triangular_solve(lower, identity, left_side=True, lower=True)]
    another operation x26 -> x0, matrix products: 22.9 us -> none  [the longest x14 12 us: factorize(): lax.linalg.triangular_solve(lower, identity, left_side=True, lower=True)]
    slice x8 -> x1, local copies, waits for them, and re-layouts: 21.5 us -> 0.74 us  [edge(): courant_y[b:b + 1]]
    sub x2, other arithmetic: 17.9 us -> 0.02 us  [the longest x1 0.01 us: body(): diffusion_number - cx]
  transfers between devices with their start and end apart: 6 -> 2, of which waited for: 2 -> 1; matrix products, arithmetic and copies ran while one was open for 5% -> 0% of each run, Pallas kernels for 0% -> 0%
where the time goes in v1:
time: 167 us; the launch traced here: 166 us
  Pallas kernels  146 us (87%)
  local copies, waits for them, and re-layouts  6.94 us (4%)
  waiting for transfers between devices  6.77 us (4%)
  starting transfers between devices  5.56 us (3%)
    pallas_call x2, Pallas kernels, all_reduce(): pl.pallas_call(functools.partial(reduce_kernel, n), out_shape=jax.ShapeDt...  49 us
    pallas_call x1, Pallas kernels, body(): plain(functools.partial(first_kernel, cells), [square, (vectors, width),...  41.9 us
    pallas_call x1, Pallas kernels, body(): plain(functools.partial(second_kernel, cells), [(vectors * nx, ny), squar...  33.3 us
    pallas_call x1, Pallas kernels, body(): plain(advance_kernel, [(vectors, width), (total, T)], 4)  21.9 us
    ppermute x1, waiting for transfers between devices, body(): lax.ppermute(edge(nx - 2, nx - 1), 'space', [(i, (i + 1) % n) for i in ra...  6.77 us
    ppermute x1, starting transfers between devices, body(): lax.ppermute(edge(0, 0), 'space', [((i + 1) % n, i) for i in range(n)])  5.06 us
  transfers between devices with their start and end apart: 2, of which 1 were waited for; matrix products, arithmetic and copies ran while one was open for 0% of the time, Pallas kernels for 0%

profile of v1, /device:TPU:0, one launch (start us, length us, event | category | flops | bytes accessed | tf_op | source)
XLA Modules:
  0.0 166.1 jit_solution(11510875480410511664)
XLA Ops:
  0.6 0.0 copy-start.3
  0.6 0.0 copy-start.2
  0.7 2.6 %slice_bitcast_fusion = (f32[2,512,128]{2,0,1:T(2,128)S(1)}, f32[2,512,128]{2,0,1:T(2,128)S(1)}) fusion(f32[512,16,128]{2,1,0:T(8,128)} %param.3), kind=kLoop, calls=%fused_computation | loop fusion | bytes 2097152 | tf_op jit(solution)/shard_map/transpose | solution.py:330
  3.3 0.7 fusion.4
  4.0 0.1 concatenate.46
  4.2 0.5 collective-permute-start
  4.7 0.1 concatenate.47
  4.9 5.1 %collective-permute-start.1 = (f32[1032,128]{1,0:T(8,128)S(1)}, f32[1032,128]{1,0:T(8,128)S(1)}, u32[]{:S(2)}, u32[]{:S(2)}) collective-permute-start(f32[1032,128]{1,0:T(8,128)S(1)} %concatenate.47), channel_id=1, source_target_pairs={{1,0},{2,1},{3,2},{4,3},{5,4},{6,5},{7,6},{8,7},{9,8},{10,9},{11,1... | collective-permute-start | bytes 1585160 | tf_op jit(solution)/shard_map/ppermute | solution.py:334
  9.9 6.8 %collective-permute-done.low_ref = f32[1032,128]{1,0:T(8,128)S(1)} collective-permute-done((f32[1032,128]{1,0:T(8,128)S(1)}, f32[1032,128]{1,0:T(8,128)S(1)}, u32[]{:S(2)}, u32[]{:S(2)}) %collective-permute-start) | collective-permute-done | bytes 528416 | tf_op jit(solution)/shard_map/ppermute | solution.py:333
  16.7 0.0 collective-permute-done.1.high_ref
  16.7 0.0 copy-done.2
  16.7 0.0 copy-done.3
  16.8 21.9 %shard_map.66 = (f32[512,2048]{1,0:T(8,128)S(1)}, f32[1280,128]{1,0:T(8,128)S(1)}) custom-call(f32[8192,128]{1,0:T(8,128)} %bitcast.19, f32[1032,128]{1,0:T(8,128)S(1)} %collective-permute-done.low_ref, f32[1032,128]{1,0:T(8,128)S(1)} %collective-permute-done.1.high_ref, f32[4,18,128]{2,1,0:T(8,128)S(1)} %pad_maximum_fusion.coef_ref), custom_call_target="tpu_custom_call" | custom-call | tf_op jit(solution)/shard_map/pallas_call | solution.py:340
  38.7 0.0 copy-start
  38.7 2.0 %copy-done = f32[512,2048]{1,0:T(8,128)} copy-done((f32[512,2048]{1,0:T(8,128)}, f32[512,2048]{1,0:T(8,128)S(1)}, u32[]{:S(2)}) %copy-start) | copy-done | bytes 4194328
  40.7 25.6 %shard_map.67.packed_ref = f32[1280,128]{1,0:T(8,128)S(1)} custom-call(f32[1280,128]{1,0:T(8,128)S(1)} %get-tuple-element.12.x_ref), custom_call_target="tpu_custom_call" | custom-call | tf_op jit(solution)/shard_map/pallas_call | solution.py:307
  66.3 41.9 %shard_map.68 = (f32[512,512]{1,0:T(8,128)}, f32[512,2048]{1,0:T(8,128)S(1)}, f32[1280,128]{1,0:T(8,128)S(1)}) custom-call(f32[1280,128]{1,0:T(8,128)S(1)} %shard_map.67.packed_ref, f32[512,2048]{1,0:T(8,128)} %copy-done), custom_call_target="tpu_custom_call" | custom-call | tf_op jit(solution)/shard_map/pallas_call | solution.py:345
  108.2 23.4 %shard_map.69.packed_ref = f32[1280,128]{1,0:T(8,128)S(1)} custom-call(f32[1280,128]{1,0:T(8,128)S(1)} %get-tuple-element.14.x_ref), custom_call_target="tpu_custom_call" | custom-call | tf_op jit(solution)/shard_map/pallas_call | solution.py:307
  131.6 0.0 copy-start.1
  131.6 1.2 copy-done.1
  132.8 33.3 %shard_map.70 = (f32[8192,128]{1,0:T(8,128)}, f32[512,512]{1,0:T(8,128)}, f32[4,128]{1,0:T(4,128)}) custom-call(f32[1280,128]{1,0:T(8,128)S(1)} %shard_map.69.packed_ref, f32[512,2048]{1,0:T(8,128)S(1)} %get-tuple-element.15.q_ref, f32[512,512]{1,0:T(8,128)S(1)} %copy-done.1), custom_call_target="tpu_custom_call" | custom-call | tf_op jit(solution)/shard_map/pallas_call | solution.py:349
  (8 shorter events, 0.1 us)
Async XLA Ops:
  0.6 16.1 %copy-start.3 = (f32[16,128]{1,0:T(8,128)S(1)}, f32[16,128]{1,0:T(8,128)}, u32[]{:S(2)}) copy-start(f32[16,128]{1,0:T(8,128)} %param.5) | copy-start | bytes 24580
  0.6 16.1 %copy-start.2 = (f32[16,128]{1,0:T(8,128)S(1)}, f32[16,128]{1,0:T(8,128)}, u32[]{:S(2)}) copy-start(f32[16,128]{1,0:T(8,128)} %param.4) | copy-start | bytes 24580
  4.2 12.5 %collective-permute-start = (f32[1032,128]{1,0:T(8,128)S(1)}, f32[1032,128]{1,0:T(8,128)S(1)}, u32[]{:S(2)}, u32[]{:S(2)}) collective-permute-start(f32[1032,128]{1,0:T(8,128)S(1)} %concatenate.46), channel_id=1, source_target_pairs={{0,1},{1,2},{2,3},{3,4},{4,5},{5,6},{6,7},{7,8},{8,9},{9,10},{10,1... | collective-permute-start | bytes 1585160 | tf_op jit(solution)/shard_map/ppermute | solution.py:333
  4.9 11.8 %collective-permute-start.1 = (f32[1032,128]{1,0:T(8,128)S(1)}, f32[1032,128]{1,0:T(8,128)S(1)}, u32[]{:S(2)}, u32[]{:S(2)}) collective-permute-start(f32[1032,128]{1,0:T(8,128)S(1)} %concatenate.47), channel_id=1, source_target_pairs={{1,0},{2,1},{3,2},{4,3},{5,4},{6,5},{7,6},{8,7},{9,8},{10,9},{11,1... | collective-permute-start | bytes 1585160 | tf_op jit(solution)/shard_map/ppermute | solution.py:334
  38.7 2.0 %copy-start = (f32[512,2048]{1,0:T(8,128)}, f32[512,2048]{1,0:T(8,128)S(1)}, u32[]{:S(2)}) copy-start(f32[512,2048]{1,0:T(8,128)S(1)} %get-tuple-element.13.v_ref) | copy-start | bytes 12582916
  131.6 1.2 copy-start.1

commit v2 on v1

--- a/solution.py
+++ b/solution.py
@@ -9,6 +9,7 @@
 
 diffusion_number = 0.2
 T = 128
+B = 256
 MICRO = 16
 HIGHEST = lax.Precision.HIGHEST
 MESH = pl.DeviceIdType.MESH
@@ -35,57 +36,171 @@
     return chunk, chunk * devices
 
 
-def gram_into(v_ref, packed_ref):
+def split(value):
+    high = value.astype(jnp.bfloat16)
+    rest = value - high.astype(jnp.float32)
+    middle = rest.astype(jnp.bfloat16)
+    low = (rest - middle.astype(jnp.float32)).astype(jnp.bfloat16)
+    return high, middle, low
+
+
+def parts_left(high, middle, low, axis):
+    return jnp.concatenate([low, high, middle, middle, high, high], axis=axis)
+
+
+def parts_right(high, middle, low, axis):
+    return jnp.concatenate([high, low, middle, high, middle, high], axis=axis)
+
+
+def product(a, b, dims):
+    return lax.dot_general(a, b, (dims, ((), ())), preferred_element_type=jnp.float32)
+
+
+def gram_into(v_refs, acc_ref):
+    vectors = v_refs[0].shape[0]
+    wide = vectors // B
+    acc_ref[...] = jnp.zeros_like(acc_ref)
+    for v_ref in v_refs:
+
+        def step(s, _):
+            cols = pl.ds(pl.multiple_of(s * B, B), B)
+            parts = [split(v_ref[i * B:(i + 1) * B, cols]) for i in range(wide)]
+            at = 0
+            for i in range(wide):
+                high, middle, low = parts[i]
+                same = jnp.concatenate([middle, high], axis=1)
+                acc_ref[at] += product(same, same, NT)
+                mixed = jnp.concatenate([low, middle], axis=1)
+                acc_ref[at + 1] += product(jnp.concatenate([high, high], axis=1), mixed, NT)
+                at += 2
+            for i in range(wide):
+                for j in range(i + 1, wide):
+                    acc_ref[at] += product(parts_left(*parts[i], 1), parts_right(*parts[j], 1), NT)
+                    at += 1
+            return 0
+
+        lax.fori_loop(0, v_ref.shape[1] // B, step, 0)
+
+
+def gram_scratch(vectors):
+    wide = vectors // B
+    return (2 * wide + wide * (wide - 1) // 2, B, B)
+
+
+def pack(acc_ref, packed_ref, vectors, add_ref=None):
+    wide = vectors // B
+    blocks = {}
+    for i in range(wide):
+        mixed = acc_ref[2 * i + 1]
+        blocks[i, i] = acc_ref[2 * i] + (mixed + mixed.T)
+    at = 2 * wide
+    for i in range(wide):
+        for j in range(i + 1, wide):
+            blocks[i, j] = acc_ref[at]
+            at += 1
+    r = B // T
+    end = 0
+    for i, j in pair_list(vectors // T):
+        value = blocks[i // r, j // r][i % r * T:(i % r + 1) * T, j % r * T:(j % r + 1) * T]
+        if add_ref is not None:
+            value = value + add_ref[end:end + T, :]
+        packed_ref[end:end + T, :] = value
+        end += T
+    if end < packed_ref.shape[0]:
+        packed_ref[end:, :] = jnp.zeros((packed_ref.shape[0] - end, T), jnp.float32)
+
+
+def lower_times(inverse_ref, split_refs, v_ref, emit):
     vectors, width = v_ref.shape
-    blocks = vectors // T
-    packed_ref[...] = jnp.zeros_like(packed_ref)
+    wide = vectors // B
 
     def step(s, _):
-        cols = pl.ds(pl.multiple_of(s * 256, 256), 256)
-        at = 0
-        for i in range(blocks):
-            left = v_ref[i * T:(i + 1) * T, cols]
-            for j in range(i, blocks):
-                packed_ref[at:at + T, :] += dot(left, v_ref[j * T:(j + 1) * T, cols], NT)
-                at += T
-        return 0
-
-    lax.fori_loop(0, width // 256, step, 0)
-
-
-def advance_kernel(w_ref, low_ref, high_ref, coef_ref, v_ref, packed_ref):
+        cols = pl.ds(pl.multiple_of(s * B, B), B)
+        parts = [parts_right(*split(v_ref[k * B:(k + 1) * B, cols]), 0) for k in range(wide)]
+        for i in range(wide):
+            total = None
+            for k in range(i + 1):
+                left = parts_left(*[ref[i * B:(i + 1) * B, k * B:(k + 1) * B] for ref in split_refs], 1)
+                term = product(left, parts[k], NN)
+                total = term if total is None else total + term
+            emit(i, s, cols, total)
+        return 0
+
+    lax.fori_loop(0, width // B, step, 0)
+
+
+def split_into(inverse_ref, split_refs):
+    for i in range(inverse_ref.shape[0] // T):
+        here = slice(i * T, (i + 1) * T)
+        for ref, value in zip(split_refs, split(inverse_ref[here, :])):
+            ref[here, :] = value
+
+
+def apply(west, center, east, coef_ref, e):
+    ce, cw, cn, cs = [coef_ref[f, e:e + 1, :] for f in range(4)]
+    north = pltpu.roll(center, T - 1, 1)
+    south = pltpu.roll(center, 1, 1)
+    return ((1.0 - 4.0 * diffusion_number) * center + (ce * east + cw * west)) + (cn * north + cs * south)
+
+
+def two_steps(row, first, count, coef_ref, coef_at, store):
+    zero = [row(first - 2), row(first - 1)]
+    one = []
+    for x in range(first - 1, first + count + 1):
+        zero.append(row(x + 1))
+        one.append(apply(*zero[-3:], coef_ref, coef_at(x)))
+        if len(one) >= 3:
+            store(x - 1, apply(*one[-3:], coef_ref, coef_at(x - 1)))
+
+
+def interior_kernel(w_ref, coef_ref, v_ref, packed_ref, acc_ref):
     vectors = v_ref.shape[0]
-    nx = v_ref.shape[1] // T
+    nx = v_ref.shape[1] // T + 4
     kc = 32
 
     def step(s, _):
         k0 = pl.multiple_of(s * kc, kc)
 
-        def row(e):
-            if e < 2:
-                return low_ref[pl.ds(e * vectors + k0, kc), :]
-            if e >= nx + 2:
-                return high_ref[pl.ds((e - nx - 2) * vectors + k0, kc), :]
-            return w_ref[pl.ds(k0 * nx + (e - 2), kc, stride=nx), :]
-
-        def apply(west, center, east, e):
-            ce, cw, cn, cs = [coef_ref[f, e - 1:e, :] for f in range(4)]
-            north = pltpu.roll(center, T - 1, 1)
-            south = pltpu.roll(center, 1, 1)
-            return ((1.0 - 4.0 * diffusion_number) * center + (ce * east + cw * west)) + (cn * north + cs * south)
-
-        zero = [row(0), row(1)]
-        one = []
-        for e in range(1, nx + 3):
-            zero.append(row(e + 1))
-            one.append(apply(zero[-3], zero[-2], zero[-1], e))
-            if e >= 3:
-                x = e - 3
-                v_ref[pl.ds(k0, kc), x * T:(x + 1) * T] = apply(one[-3], one[-2], one[-1], e - 1)
+        def row(x):
+            return w_ref[pl.ds(k0 * nx + x, kc, stride=nx), :]
+
+        def store(x, value):
+            v_ref[pl.ds(k0, kc), (x - 2) * T:(x - 1) * T] = value
+
+        two_steps(row, 2, nx - 4, coef_ref, lambda x: x, store)
         return 0
 
     lax.fori_loop(0, vectors // kc, step, 0)
-    gram_into(v_ref, packed_ref)
+    gram_into([v_ref], acc_ref)
+    pack(acc_ref, packed_ref, vectors)
+
+
+def edge_kernel(nx, mine_ref, low_ref, high_ref, coef_ref, add_ref, v_ref, packed_ref, acc_ref):
+    vectors = v_ref.shape[0]
+    kc = 32
+
+    def step(s, _):
+        k0 = pl.multiple_of(s * kc, kc)
+
+        def row(x):
+            if x < 0:
+                return low_ref[pl.ds((x + 2) * vectors + k0, kc), :]
+            if x >= nx:
+                return high_ref[pl.ds((x - nx) * vectors + k0, kc), :]
+            at = x if x < 4 else x - nx + 8
+            return mine_ref[pl.ds(at * vectors + k0, kc), :]
+
+        def store(x, value):
+            at = x if x < 2 else x - nx + 4
+            v_ref[pl.ds(k0, kc), at * T:(at + 1) * T] = value
+
+        two_steps(row, 0, 2, coef_ref, lambda x: x + 1, store)
+        two_steps(row, nx - 2, 2, coef_ref, lambda x: x + 1, store)
+        return 0
+
+    lax.fori_loop(0, vectors // kc, step, 0)
+    gram_into([v_ref], acc_ref)
+    pack(acc_ref, packed_ref, vectors, add_ref)
 
 
 def eliminate(block):
@@ -150,36 +265,36 @@
     lax.fori_loop(0, blocks, step, 0)
 
 
-def first_kernel(cells, packed_ref, v_ref, upper_ref, q_ref, out_ref, z_ref, row_ref, inverse_ref):
-    vectors, width = v_ref.shape
+def first_kernel(cells, packed_ref, inner_ref, outer_ref, upper_ref, q_inner_ref, q_outer_ref, out_ref, z_ref, row_ref, inverse_ref, acc_ref, *split_refs):
+    vectors = inner_ref.shape[0]
     factor_into(packed_ref, cells, z_ref, row_ref, upper_ref, inverse_ref)
-
-    def step(s, _):
-        cols = pl.ds(pl.multiple_of(s * 256, 256), 256)
-        for i in range(vectors // T):
-            q_ref[i * T:(i + 1) * T, cols] = dot(
-                inverse_ref[i * T:(i + 1) * T, :(i + 1) * T], v_ref[:(i + 1) * T, cols], NN
-            )
-        return 0
-
-    lax.fori_loop(0, width // 256, step, 0)
-    gram_into(q_ref, out_ref)
-
-
-def second_kernel(cells, packed_ref, q_ref, first_ref, basis_ref, growth_ref, log_ref, z_ref, row_ref, inverse_ref, upper_ref):
-    vectors, width = q_ref.shape
-    nx = width // T
+    split_into(inverse_ref, split_refs)
+    for v_ref, q_ref in ((inner_ref, q_inner_ref), (outer_ref, q_outer_ref)):
+
+        def emit(i, s, cols, value):
+            q_ref[i * B:(i + 1) * B, cols] = value
+
+        lower_times(inverse_ref, split_refs, v_ref, emit)
+    gram_into([q_inner_ref, q_outer_ref], acc_ref)
+    pack(acc_ref, out_ref, vectors)
+
+
+def second_kernel(cells, packed_ref, inner_ref, outer_ref, first_ref, basis_ref, growth_ref, log_ref, z_ref, row_ref, inverse_ref, upper_ref, *split_refs):
+    vectors = inner_ref.shape[0]
+    nx = basis_ref.shape[0] // vectors
     factor_into(packed_ref, cells, z_ref, row_ref, upper_ref, inverse_ref)
-
-    def step(s, _):
-        cols = pl.ds(pl.multiple_of(s * 256, 256), 256)
-        for i in range(vectors // T):
-            value = dot(inverse_ref[i * T:(i + 1) * T, :(i + 1) * T], q_ref[:(i + 1) * T, cols], NN)
-            for h in range(2):
-                basis_ref[pl.ds(i * T * nx + 2 * s + h, T, stride=nx), :] = value[:, h * T:(h + 1) * T]
-        return 0
-
-    lax.fori_loop(0, width // 256, step, 0)
+    split_into(inverse_ref, split_refs)
+
+    def emit_inner(i, s, cols, value):
+        for h in range(2):
+            basis_ref[pl.ds(i * B * nx + 2 + 2 * s + h, B, stride=nx), :] = value[:, h * T:(h + 1) * T]
+
+    def emit_outer(i, s, cols, value):
+        for h in range(2):
+            basis_ref[pl.ds(i * B * nx + s * (nx - 2) + h, B, stride=nx), :] = value[:, h * T:(h + 1) * T]
+
+    lower_times(inverse_ref, split_refs, inner_ref, emit_inner)
+    lower_times(inverse_ref, split_refs, outer_ref, emit_outer)
     rows = lax.broadcasted_iota(jnp.int32, (T, T), 0)
     lanes = lax.broadcasted_iota(jnp.int32, (T, T), 1)
     for i in range(vectors // T):
@@ -218,12 +333,14 @@
 
     mine = pl.multiple_of(core * half, 8)
     other = pl.multiple_of((1 - core) * half, 8)
-    swap = pltpu.make_async_remote_copy(
-        src_ref=x_ref.at[pl.ds(other, half)], dst_ref=pair_buf, send_sem=pair_s, recv_sem=pair_r,
-        device_id={"space": partner}, device_id_type=MESH)
-    swap.start()
-    swap.wait()
-    sum_buf[...] = x_ref[pl.ds(mine, half), :] + pair_buf[...]
+
+    def swap(k):
+        at = lax.rem(chip + k, chips) * chunk
+        return pltpu.make_async_remote_copy(
+            src_ref=x_ref.at[pl.ds(pl.multiple_of(other + at, 8), chunk)],
+            dst_ref=pair_buf.at[pl.ds(pl.multiple_of(at, 8), chunk)],
+            send_sem=pair_s.at[k], recv_sem=pair_r.at[k],
+            device_id={"space": partner}, device_id_type=MESH)
 
     def scatter(k):
         to = lax.rem(chip + k, chips)
@@ -231,11 +348,27 @@
             src_ref=sum_buf.at[pl.ds(pl.multiple_of(to * chunk, 8), chunk)], dst_ref=recv_buf.at[k],
             send_sem=rs_s.at[k], recv_sem=rs_r.at[k], device_id={"space": peer(k)}, device_id_type=MESH)
 
-    def start_scatter(k, _):
+    def start_swap(k, _):
+        swap(lax.rem(k, chips)).start()
+        return 0
+
+    lax.fori_loop(1, chips + 1, start_swap, 0)
+
+    def start_scatter(i, _):
+        k = lax.rem(i, chips)
+        swap(k).wait_recv()
+        at = lax.rem(chip + k, chips) * chunk
+        here = pl.ds(pl.multiple_of(at, 8), chunk)
+        sum_buf[here, :] = x_ref[pl.ds(pl.multiple_of(mine + at, 8), chunk), :] + pair_buf[here, :]
+        return 0
+
+    def send_on(k, _):
+        start_scatter(k, 0)
         scatter(k).start()
         return 0
 
-    lax.fori_loop(1, chips, start_scatter, 0)
+    lax.fori_loop(1, chips, send_on, 0)
+    start_scatter(0, 0)
     own = pl.ds(pl.multiple_of(chip * chunk, 8), chunk)
     own_out = pl.ds(pl.multiple_of(mine + chip * chunk, 8), chunk)
 
@@ -276,6 +409,12 @@
 
     lax.fori_loop(0, chips, finish, 0)
 
+    def drain_swap(k, _):
+        swap(k).wait_send()
+        return 0
+
+    lax.fori_loop(0, chips, drain_swap, 0)
+
     def drain(k, _):
         scatter(k).wait_send()
         gather(k).wait_send()
@@ -288,14 +427,18 @@
     return pl.BlockSpec(memory_space=memory)
 
 
-def plain(kernel, outs, ins, scratch=()):
+def plain(kernel, outs, ins, scratch=(), splits=0, cost=None):
+    scratch_shapes = [pltpu.VMEM(shape, jnp.float32) for shape in scratch]
+    if splits:
+        scratch_shapes += [pltpu.VMEM((splits, splits), jnp.bfloat16)] * 3
     return pl.pallas_call(
         kernel,
-        out_shape=tuple(jax.ShapeDtypeStruct(s, jnp.float32) for s in outs),
+        out_shape=tuple(jax.ShapeDtypeStruct(shape, jnp.float32) for shape in outs),
         in_specs=[whole()] * ins,
         out_specs=tuple(whole() for _ in outs),
-        scratch_shapes=[pltpu.VMEM(s, jnp.float32) for s in scratch],
+        scratch_shapes=scratch_shapes,
         compiler_params=pltpu.CompilerParams(vmem_limit_bytes=VMEM_LIMIT),
+        cost_estimate=cost,
     )
 
 
@@ -313,7 +456,7 @@
             pltpu.VMEM((half, T), jnp.float32),
             pltpu.VMEM((half, T), jnp.float32),
             pltpu.VMEM((chips, half // chips, T), jnp.float32),
-            sems, sems,
+            sems((chips,)), sems((chips,)),
             sems((chips,)), sems((chips,)), sems((chips,)), sems((chips,)), sems((chips,)), sems((chips,)),
         ],
         compiler_params=pltpu.CompilerParams(collective_id=0, has_side_effects=True, vmem_limit_bytes=VMEM_LIMIT),
@@ -326,30 +469,41 @@
     width = nx * ny
     cells = float(width * n)
 
+    pick = jnp.concatenate([tangent[:, :4], tangent[:, nx - 4:]], axis=1)
+    mine = jnp.transpose(pick, (1, 0, 2)).reshape(8 * vectors, ny)
+
     def edge(a, b):
-        rows = jnp.transpose(tangent[:, a:a + 2], (1, 0, 2)).reshape(2 * vectors, ny)
+        rows = mine[a * vectors:(a + 2) * vectors]
         return jnp.concatenate([rows, courant_x[b:b + 1], courant_y[b:b + 1], jnp.zeros((6, ny), jnp.float32)], axis=0)
 
-    low = lax.ppermute(edge(nx - 2, nx - 1), "space", [(i, (i + 1) % n) for i in range(n)])
+    def coefficients(x, y):
+        x, y = 0.5 * x, 0.5 * y
+        return jnp.stack([diffusion_number - x, diffusion_number + x, diffusion_number - y, diffusion_number + y])
+
+    low = lax.ppermute(edge(6, nx - 1), "space", [(i, (i + 1) % n) for i in range(n)])
     high = lax.ppermute(edge(0, 0), "space", [((i + 1) % n, i) for i in range(n)])
     e = 2 * vectors
-    cx = 0.5 * jnp.concatenate([low[e:e + 1], courant_x, high[e:e + 1]], axis=0)
-    cy = 0.5 * jnp.concatenate([low[e + 1:e + 2], courant_y, high[e + 1:e + 2]], axis=0)
-    coef = jnp.stack([diffusion_number - cx, diffusion_number + cx, diffusion_number - cy, diffusion_number + cy])
+    cx = jnp.concatenate([low[e:e + 1], courant_x, high[e:e + 1]], axis=0)
+    cy = jnp.concatenate([low[e + 1:e + 2], courant_y, high[e + 1:e + 2]], axis=0)
     total = gram_rows(vectors, n)[1]
-    v, packed = plain(advance_kernel, [(vectors, width), (total, T)], 4)(
-        tangent.reshape(vectors * nx, ny), low, high, coef)
+    inner, outer = (vectors, width - 4 * ny), (vectors, 4 * ny)
+    acc = gram_scratch(vectors)
+    cost = pl.CostEstimate(flops=12 * vectors * vectors * width, bytes_accessed=12 * vectors * width, transcendentals=0)
+    v_inner, part = plain(interior_kernel, [inner, (total, T)], 2, [acc], cost=cost)(
+        tangent.reshape(vectors * nx, ny), coefficients(courant_x, courant_y))
+    v_outer, packed = plain(functools.partial(edge_kernel, nx), [outer, (total, T)], 5, [acc])(
+        mine, low, high, coefficients(cx, cy), part)
     packed = all_reduce(packed, n)
     square = (vectors, vectors)
     row = (T, vectors)
-    first_upper, q, packed = plain(
-        functools.partial(first_kernel, cells), [square, (vectors, width), (total, T)], 2, [square, row, square],
-    )(packed, v)
+    first_upper, q_inner, q_outer, packed = plain(
+        functools.partial(first_kernel, cells), [square, inner, outer, (total, T)], 3, [square, row, square, acc], vectors,
+    )(packed, v_inner, v_outer)
     packed = all_reduce(packed, n)
     basis, growth, log_growth = plain(
-        functools.partial(second_kernel, cells), [(vectors * nx, ny), square, (vectors // T, T)], 3,
-        [square, row, square, square],
-    )(packed, q, first_upper)
+        functools.partial(second_kernel, cells), [(vectors * nx, ny), square, (vectors // T, T)], 4,
+        [square, row, square, square], vectors,
+    )(packed, q_inner, q_outer, first_upper)
     return basis.reshape(tangent.shape), growth, log_growth.reshape(vectors), first_upper
 
 

time: 167 us -> 154 us (0.922)
  Pallas kernels: 146 us -> 133 us
  waiting for transfers between devices: 6.77 us -> 0.01 us
  local copies, waits for them, and re-layouts: 6.94 us -> 13 us
    ppermute x1, waiting for transfers between devices: 6.77 us -> 0.01 us  [body(): lax.ppermute(edge(6, nx - 1), 'space', [(i, (i + 1) % n) for i in range(n)])]
    pallas_call x2, Pallas kernels: 49 us -> 42.5 us  [all_reduce(): pl.pallas_call(functools.partial(reduce_kernel, n), out_shape=jax.ShapeDt...]
    pallas_call x2 -> x3, Pallas kernels: 63.7 us -> 57.4 us  [the longest x1 38.9 us: body(): plain(functools.partial(first_kernel, cells), [square, inner, outer, (tot...]
    slice x0 -> x4, local copies, waits for them, and re-layouts: none -> 4.8 us  [the longest x1 2.59 us: body(): pick = jnp.concatenate([tangent[:, :4], tangent[:, nx - 4:]], axis=1)]
    concatenate x2, local copies, waits for them, and re-layouts: 0.29 us -> 2.95 us  [edge(): jnp.concatenate([rows, courant_x[b:b + 1], courant_y[b:b + 1], jnp.zeros(...]
    transpose x3 -> x1, local copies, waits for them, and re-layouts: 2.66 us -> 0.41 us  [body(): mine = jnp.transpose(pick, (1, 0, 2)).reshape(8 * vectors, ny)]
    unnamed x8 -> x10, local copies, waits for them, and re-layouts: 3.24 us -> 4.78 us
  transfers between devices with their start and end apart: 2 -> 2, of which waited for: 1 -> 0; matrix products, arithmetic and copies ran while one was open for 0% -> 2% of each run, Pallas kernels for 0% -> 9%
where the time goes in v2:
time: 154 us; the launch traced here: 153 us
  Pallas kernels  133 us (86%)
  local copies, waits for them, and re-layouts  13 us (8%)
  starting transfers between devices  5.45 us (4%)
    pallas_call x2, Pallas kernels, all_reduce(): pl.pallas_call(functools.partial(reduce_kernel, n), out_shape=jax.ShapeDt...  42.5 us
    pallas_call x1, Pallas kernels, body(): plain(functools.partial(first_kernel, cells), [square, inner, outer, (tot...  38.9 us
    pallas_call x1, Pallas kernels, body(): plain(functools.partial(second_kernel, cells), [(vectors * nx, ny), squar...  33.2 us
    pallas_call x1, Pallas kernels, body(): plain(interior_kernel, [inner, (total, T)], 2, [acc], cost=cost)  13.8 us
    ppermute x1, starting transfers between devices, body(): lax.ppermute(edge(0, 0), 'space', [((i + 1) % n, i) for i in range(n)])  4.99 us
    unnamed x10, local copies, waits for them, and re-layouts  4.78 us
    pallas_call x1, Pallas kernels, body(): plain(functools.partial(edge_kernel, nx), [outer, (total, T)], 5, [acc])  4.73 us
  transfers between devices with their start and end apart: 2, of which 0 were waited for; matrix products, arithmetic and copies ran while one was open for 2% of the time, Pallas kernels for 9%

profile of v2, /device:TPU:0, one launch (start us, length us, event | category | flops | bytes accessed | tf_op | source)
XLA Modules:
  0.0 152.7 jit_solution(17624041274221418767)
XLA Ops:
  0.6 2.6 %fusion.4 = (f32[512,4,128]{2,1,0:T(4,128)S(1)}, f32[512,4,128]{2,1,0:T(4,128)S(1)}) fusion(f32[512,16,128]{2,1,0:T(8,128)} %param.3), kind=kLoop, calls=%fused_computation.17 | loop fusion | bytes 4194304 | tf_op jit(solution)/shard_map/slice | solution.py:472
  3.2 0.4 maximum_bitcast_fusion
  3.6 0.0 copy-start.3
  3.6 0.0 copy-start.4
  3.7 1.1 fusion.5
  4.8 0.0 copy-done.3
  4.8 0.0 copy-done.4
  4.9 1.5 concatenate.50
  6.3 0.5 collective-permute-start
  6.8 1.1 copy.9
  7.9 1.5 concatenate.51
  9.3 5.0 %collective-permute-start.1 = (f32[1032,128]{1,0:T(8,128)}, f32[1032,128]{1,0:T(8,128)S(1)}, u32[]{:S(2)}, u32[]{:S(2)}) collective-permute-start(f32[1032,128]{1,0:T(8,128)} %concatenate.51), channel_id=1, source_target_pairs={{1,0},{2,1},{3,2},{4,3},{5,4},{6,5},{7,6},{8,7},{9,8},{10,9},{11,1... | collective-permute-start | bytes 1585160 | tf_op jit(solution)/shard_map/ppermute | solution.py:484
  14.3 0.4 copy.7
  14.8 13.8 %shard_map.66 = (f32[512,1536]{1,0:T(8,128)S(1)}, f32[1280,128]{1,0:T(8,128)S(1)}) custom-call(f32[8192,128]{1,0:T(8,128)} %bitcast.29, f32[4,16,128]{2,1,0:T(8,128)S(1)} %pad_maximum_fusion.1.coef_ref), custom_call_target="tpu_custom_call" | custom-call | flops 6442450944 | bytes 12582912 | tf_op jit(solution)/shard_map/pallas_call | solution.py:492
  28.6 0.0 copy-start
  28.6 1.7 %copy-done = f32[512,1536]{1,0:T(8,128)} copy-done((f32[512,1536]{1,0:T(8,128)}, f32[512,1536]{1,0:T(8,128)S(1)}, u32[]{:S(2)}) %copy-start) | copy-done | bytes 3145752
  30.3 0.0 collective-permute-done.low_ref
  30.3 0.0 collective-permute-done.1.high_ref
  30.3 4.7 %shard_map.67 = (f32[512,512]{1,0:T(8,128)S(1)}, f32[1280,128]{1,0:T(8,128)S(1)}) custom-call(f32[4096,128]{1,0:T(8,128)S(1)} %bitcast.26, f32[1032,128]{1,0:T(8,128)S(1)} %collective-permute-done.low_ref, f32[1032,128]{1,0:T(8,128)S(1)} %collective-permute-done.1.high_ref, f32[4,18,128]{2,1,0:T(8,128)S(1)} %pad_maximum_fusion.coef_ref, ...), custom_call_target="tpu_custom_call" | custom-call | tf_op jit(solution)/shard_map/pallas_call | solution.py:494
  35.1 18.8 %shard_map.68.packed_ref = f32[1280,128]{1,0:T(8,128)S(1)} custom-call(f32[1280,128]{1,0:T(8,128)S(1)} %get-tuple-element.16.x_ref), custom_call_target="tpu_custom_call" | custom-call | tf_op jit(solution)/shard_map/pallas_call | solution.py:450
  53.9 38.9 %shard_map.69 = (f32[512,512]{1,0:T(8,128)}, f32[512,1536]{1,0:T(8,128)}, f32[512,512]{1,0:T(8,128)S(1)}, f32[1280,128]{1,0:T(8,128)S(1)}) custom-call(f32[1280,128]{1,0:T(8,128)S(1)} %shard_map.68.packed_ref, f32[512,1536]{1,0:T(8,128)} %copy-done, f32[512,512]{1,0:T(8,128)S(1)} %get-tuple-element.18.outer_ref), custom_call_target="tpu_custom_call" | custom-call | tf_op jit(solution)/shard_map/pallas_call | solution.py:499
  92.8 23.6 %shard_map.70.packed_ref = f32[1280,128]{1,0:T(8,128)S(1)} custom-call(f32[1280,128]{1,0:T(8,128)S(1)} %get-tuple-element.19.x_ref), custom_call_target="tpu_custom_call" | custom-call | tf_op jit(solution)/shard_map/pallas_call | solution.py:450
  116.4 0.0 copy-start.1
  116.4 1.9 %copy-done.1 = f32[512,1536]{1,0:T(8,128)S(1)} copy-done((f32[512,1536]{1,0:T(8,128)S(1)}, f32[512,1536]{1,0:T(8,128)}, u32[]{:S(2)}) %copy-start.1) | copy-done | bytes 3145752
  118.3 0.0 copy-start.2
  118.3 1.2 copy-done.2
  119.5 33.2 %shard_map.71 = (f32[8192,128]{1,0:T(8,128)}, f32[512,512]{1,0:T(8,128)}, f32[4,128]{1,0:T(4,128)}) custom-call(f32[1280,128]{1,0:T(8,128)S(1)} %shard_map.70.packed_ref, f32[512,1536]{1,0:T(8,128)S(1)} %copy-done.1, f32[512,512]{1,0:T(8,128)S(1)} %get-tuple-element.21.outer_ref, f32[512,512]{1,0:T(8,128)S(1)} %copy-done.2), custom_call_target="tpu_custom_call" | custom-call | tf_op jit(solution)/shard_map/pallas_call | solution.py:503
  (10 shorter events, 0.1 us)
Async XLA Ops:
  3.6 1.2 copy-start.3
  3.6 1.2 copy-start.4
  6.3 23.9 %collective-permute-start = (f32[1032,128]{1,0:T(8,128)}, f32[1032,128]{1,0:T(8,128)S(1)}, u32[]{:S(2)}, u32[]{:S(2)}) collective-permute-start(f32[1032,128]{1,0:T(8,128)} %concatenate.50), channel_id=1, source_target_pairs={{0,1},{1,2},{2,3},{3,4},{4,5},{5,6},{6,7},{7,8},{8,9},{9,10},{10,1... | collective-permute-start | bytes 1585160 | tf_op jit(solution)/shard_map/ppermute | solution.py:483
  9.3 20.9 %collective-permute-start.1 = (f32[1032,128]{1,0:T(8,128)}, f32[1032,128]{1,0:T(8,128)S(1)}, u32[]{:S(2)}, u32[]{:S(2)}) collective-permute-start(f32[1032,128]{1,0:T(8,128)} %concatenate.51), channel_id=1, source_target_pairs={{1,0},{2,1},{3,2},{4,3},{5,4},{6,5},{7,6},{8,7},{9,8},{10,9},{11,1... | collective-permute-start | bytes 1585160 | tf_op jit(solution)/shard_map/ppermute | solution.py:484
  28.6 1.7 %copy-start = (f32[512,1536]{1,0:T(8,128)}, f32[512,1536]{1,0:T(8,128)S(1)}, u32[]{:S(2)}) copy-start(f32[512,1536]{1,0:T(8,128)S(1)} %get-tuple-element.17.inner_ref) | copy-start | bytes 9437188
  116.4 1.9 %copy-start.1 = (f32[512,1536]{1,0:T(8,128)S(1)}, f32[512,1536]{1,0:T(8,128)}, u32[]{:S(2)}) copy-start(f32[512,1536]{1,0:T(8,128)} %get-tuple-element.20.inner_ref) | copy-start | bytes 9437188
  118.3 1.2 copy-start.2

commit v3 on v2

--- a/solution.py
+++ b/solution.py
@@ -230,12 +230,13 @@
         uppers.append(upper)
         inverses.append(inverse)
         if p + 1 < T // m:
-            product = dot(upper, jnp.concatenate([upper, inverse], axis=1), TN)
-            rest = rest[m:] - product[(p + 1) * m:]
+            both = split(jnp.concatenate([upper, inverse], axis=1))
+            left = parts_left(*[part[:, :T] for part in both], 0)
+            rest = rest[m:] - product(left, parts_right(*both, 0), TN)[(p + 1) * m:]
     return jnp.concatenate(uppers, axis=0), jnp.concatenate(inverses, axis=0)
 
 
-def factor_into(packed_ref, cells, z_ref, row_ref, upper_ref, inverse_ref):
+def factor_into(packed_ref, cells, z_ref, row_ref, upper_ref, inverse_ref, left_ref, right_ref):
     vectors = z_ref.shape[0]
     blocks = vectors // T
     z_ref[...] = jnp.zeros_like(z_ref)
@@ -246,9 +247,12 @@
     def step(b, _):
         here = pl.ds(pl.multiple_of(b * T, T), T)
         upper, inverse = eliminate(z_ref[here, here])
-        row_ref[...] = dot(inverse, z_ref[here, :], NN)
+        row_ref[...] = product(parts_left(*split(inverse), 1), parts_right(*split(z_ref[here, :]), 0), NN)
         row_ref[:, here] = inverse
         row = row_ref[...]
+        parts = split(row)
+        left_ref[...] = parts_left(*parts, 0)
+        right_ref[...] = parts_right(*parts, 0)
         upper_ref[here, :] = jnp.where(block_of > b, row, 0.0)
         upper_ref[here, here] = upper
         inverse_ref[here, :] = jnp.where(block_of <= b, row, 0.0)
@@ -256,7 +260,7 @@
         def below(c, _):
             there = pl.ds(pl.multiple_of(c * T, T), T)
             old = jnp.where(block_of == b, 0.0, z_ref[there, :])
-            z_ref[there, :] = old - dot(row_ref[:, there], row_ref[...], TN)
+            z_ref[there, :] = old - product(left_ref[:, there], right_ref[...], TN)
             return 0
 
         lax.fori_loop(b + 1, blocks, below, 0)
@@ -265,9 +269,9 @@
     lax.fori_loop(0, blocks, step, 0)
 
 
-def first_kernel(cells, packed_ref, inner_ref, outer_ref, upper_ref, q_inner_ref, q_outer_ref, out_ref, z_ref, row_ref, inverse_ref, acc_ref, *split_refs):
+def first_kernel(cells, packed_ref, inner_ref, outer_ref, upper_ref, q_inner_ref, q_outer_ref, out_ref, z_ref, row_ref, inverse_ref, acc_ref, left_ref, right_ref, *split_refs):
     vectors = inner_ref.shape[0]
-    factor_into(packed_ref, cells, z_ref, row_ref, upper_ref, inverse_ref)
+    factor_into(packed_ref, cells, z_ref, row_ref, upper_ref, inverse_ref, left_ref, right_ref)
     split_into(inverse_ref, split_refs)
     for v_ref, q_ref in ((inner_ref, q_inner_ref), (outer_ref, q_outer_ref)):
 
@@ -279,10 +283,10 @@
     pack(acc_ref, out_ref, vectors)
 
 
-def second_kernel(cells, packed_ref, inner_ref, outer_ref, first_ref, basis_ref, growth_ref, log_ref, z_ref, row_ref, inverse_ref, upper_ref, *split_refs):
+def second_kernel(cells, packed_ref, inner_ref, outer_ref, first_ref, basis_ref, growth_ref, log_ref, z_ref, row_ref, inverse_ref, upper_ref, left_ref, right_ref, *split_refs):
     vectors = inner_ref.shape[0]
     nx = basis_ref.shape[0] // vectors
-    factor_into(packed_ref, cells, z_ref, row_ref, upper_ref, inverse_ref)
+    factor_into(packed_ref, cells, z_ref, row_ref, upper_ref, inverse_ref, left_ref, right_ref)
     split_into(inverse_ref, split_refs)
 
     def emit_inner(i, s, cols, value):
@@ -305,122 +309,142 @@
         log_ref[i:i + 1, :] = jnp.log(one) + jnp.log(two)
 
 
-def reduce_kernel(n, x_ref, o_ref, pair_buf, sum_buf, recv_buf, pair_s, pair_r, rs_s, rs_r, ag_s, ag_r, fw_s, fw_r):
-    chips = n // 2
-    total = x_ref.shape[0]
-    half = total // 2
-    chunk = half // chips
+def reduce_kernel(n, x_ref, o_ref, swap_buf, y_out, y_in, z_out, z_in, sw_s, sw_r, y_s, y_r, z_s, z_r, zg_s, zg_r, yg_s, yg_r, cf_s, cf_r):
+    groups = n // 4
+    chunk = x_ref.shape[0] // n
     me = lax.axis_index("space")
-    chip = me // 2
     core = me % 2
-    partner = chip * 2 + (1 - core)
-
-    def peer(k):
-        return lax.rem(chip + k, chips) * 2 + core
+    side = (me // 2) % 2
+    group = me // 4
+    core_peer = group * 4 + side * 2 + (1 - core)
+    side_peer = group * 4 + (1 - side) * 2 + core
+
+    def to(k):
+        return lax.rem(group + k, groups)
 
     def source(k):
-        return lax.rem(chip + chips - k, chips)
+        return lax.rem(group + groups - k, groups)
+
+    def rows(c, y, g):
+        return pl.ds(pl.multiple_of(((c * 2 + y) * groups + g) * chunk, 8), chunk)
+
+    def y_of(q):
+        return q * side + (1 - q) * (1 - side)
+
+    def copy(src, dst, send, recv, device):
+        return pltpu.make_async_remote_copy(
+            src_ref=src, dst_ref=dst, send_sem=send, recv_sem=recv,
+            device_id={"space": device}, device_id_type=MESH)
+
+    def z_peer(k):
+        return to(k) * 4 + side * 2 + core
+
+    def swap(q, k):
+        at = q * groups + k
+        return copy(x_ref.at[rows(1 - core, y_of(q), to(k))], swap_buf.at[at], sw_s.at[at], sw_r.at[at], core_peer)
+
+    def across(k):
+        return copy(y_out.at[k], y_in.at[k], y_s.at[k], y_r.at[k], side_peer)
+
+    def scatter(k):
+        return copy(z_out.at[k], z_in.at[k], z_s.at[k], z_r.at[k], z_peer(k))
+
+    def gather(k):
+        own = o_ref.at[rows(core, side, group)]
+        return copy(own, own, zg_s.at[k], zg_r.at[k], z_peer(k))
+
+    def side_forward(k):
+        at = o_ref.at[rows(core, side, source(k))]
+        return copy(at, at, yg_s.at[k], yg_r.at[k], side_peer)
+
+    def core_forward(q, k):
+        at = o_ref.at[rows(core, y_of(q), source(k))]
+        sem = q * groups + k
+        return copy(at, at, cf_s.at[sem], cf_r.at[sem], core_peer)
+
+    def loop(low, high, call):
+        def step(k, _):
+            call(k)
+            return 0
+
+        lax.fori_loop(low, high, step, 0)
 
     barrier = pltpu.get_barrier_semaphore()
-    pl.semaphore_signal(barrier, inc=1, device_id={"space": partner}, device_id_type=MESH)
-
-    def greet(k, _):
-        pl.semaphore_signal(barrier, inc=1, device_id={"space": peer(k)}, device_id_type=MESH)
-        return 0
-
-    lax.fori_loop(1, chips, greet, 0)
-    pl.semaphore_wait(barrier, chips)
-
-    mine = pl.multiple_of(core * half, 8)
-    other = pl.multiple_of((1 - core) * half, 8)
-
-    def swap(k):
-        at = lax.rem(chip + k, chips) * chunk
-        return pltpu.make_async_remote_copy(
-            src_ref=x_ref.at[pl.ds(pl.multiple_of(other + at, 8), chunk)],
-            dst_ref=pair_buf.at[pl.ds(pl.multiple_of(at, 8), chunk)],
-            send_sem=pair_s.at[k], recv_sem=pair_r.at[k],
-            device_id={"space": partner}, device_id_type=MESH)
-
-    def scatter(k):
-        to = lax.rem(chip + k, chips)
-        return pltpu.make_async_remote_copy(
-            src_ref=sum_buf.at[pl.ds(pl.multiple_of(to * chunk, 8), chunk)], dst_ref=recv_buf.at[k],
-            send_sem=rs_s.at[k], recv_sem=rs_r.at[k], device_id={"space": peer(k)}, device_id_type=MESH)
-
-    def start_swap(k, _):
-        swap(lax.rem(k, chips)).start()
-        return 0
-
-    lax.fori_loop(1, chips + 1, start_swap, 0)
-
-    def start_scatter(i, _):
-        k = lax.rem(i, chips)
-        swap(k).wait_recv()
-        at = lax.rem(chip + k, chips) * chunk
-        here = pl.ds(pl.multiple_of(at, 8), chunk)
-        sum_buf[here, :] = x_ref[pl.ds(pl.multiple_of(mine + at, 8), chunk), :] + pair_buf[here, :]
-        return 0
-
-    def send_on(k, _):
-        start_scatter(k, 0)
+
+    def greet(device):
+        pl.semaphore_signal(barrier, inc=1, device_id={"space": device}, device_id_type=MESH)
+
+    greet(core_peer)
+    greet(side_peer)
+    loop(1, groups, lambda k: greet(z_peer(k)))
+    pl.semaphore_wait(barrier, groups + 1)
+
+    for q in range(2):
+        loop(1, groups + 1, lambda k: swap(q, lax.rem(k, groups)).start())
+
+    def send_across(i):
+        k = lax.rem(i, groups)
+        swap(0, k).wait_recv()
+        y_out[k] = x_ref[rows(core, 1 - side, to(k)), :] + swap_buf[k]
+        across(k).start()
+
+    loop(1, groups + 1, send_across)
+
+    def combined(k):
+        swap(1, k).wait_recv()
+        across(k).wait_recv()
+        return x_ref[rows(core, side, to(k)), :] + swap_buf[groups + k] + y_in[k]
+
+    def send_out(k):
+        z_out[k] = combined(k)
         scatter(k).start()
-        return 0
-
-    lax.fori_loop(1, chips, send_on, 0)
-    start_scatter(0, 0)
-    own = pl.ds(pl.multiple_of(chip * chunk, 8), chunk)
-    own_out = pl.ds(pl.multiple_of(mine + chip * chunk, 8), chunk)
+
+    loop(1, groups, send_out)
 
     def add(k, acc):
         scatter(k).wait_recv()
-        return acc + recv_buf[k]
-
-    o_ref[own_out, :] = lax.fori_loop(1, chips, add, sum_buf[own, :])
-
-    def gather(k):
-        return pltpu.make_async_remote_copy(
-            src_ref=o_ref.at[own_out], dst_ref=o_ref.at[own_out],
-            send_sem=ag_s.at[k], recv_sem=ag_r.at[k], device_id={"space": peer(k)}, device_id_type=MESH)
-
-    def forward(k):
-        at = pl.ds(pl.multiple_of(mine + source(k) * chunk, 8), chunk)
-        return pltpu.make_async_remote_copy(
-            src_ref=o_ref.at[at], dst_ref=o_ref.at[at],
-            send_sem=fw_s.at[k], recv_sem=fw_r.at[k], device_id={"space": partner}, device_id_type=MESH)
-
-    def start_gather(k, _):
-        gather(k).start()
-        return 0
-
-    lax.fori_loop(1, chips, start_gather, 0)
-    forward(0).start()
-
-    def pass_on(k, _):
+        return acc + z_in[k]
+
+    o_ref[rows(core, side, group), :] = lax.fori_loop(1, groups, add, combined(0))
+
+    loop(1, groups, lambda k: gather(k).start())
+    side_forward(0).start()
+    core_forward(1, 0).start()
+
+    def pass_z(k):
         gather(k).wait_recv()
-        forward(k).start()
-        return 0
-
-    lax.fori_loop(1, chips, pass_on, 0)
-
-    def finish(k, _):
-        forward(k).wait()
-        return 0
-
-    lax.fori_loop(0, chips, finish, 0)
-
-    def drain_swap(k, _):
-        swap(k).wait_send()
-        return 0
-
-    lax.fori_loop(0, chips, drain_swap, 0)
-
-    def drain(k, _):
+        side_forward(k).start()
+        core_forward(1, k).start()
+
+    loop(1, groups, pass_z)
+
+    def arrived(k):
+        there = o_ref.at[rows(core, 1 - side, source(k))]
+        return copy(there, there, yg_s.at[k], yg_r.at[k], side_peer)
+
+    def pass_side(k):
+        arrived(k).wait_recv()
+        core_forward(0, k).start()
+
+    loop(0, groups, pass_side)
+
+    def finish(k):
+        for q in range(2):
+            there = o_ref.at[rows(1 - core, y_of(q), source(k))]
+            sem = q * groups + k
+            copy(there, there, cf_s.at[sem], cf_r.at[sem], core_peer).wait_recv()
+            core_forward(q, k).wait_send()
+            swap(q, k).wait_send()
+        across(k).wait_send()
+        side_forward(k).wait_send()
+
+    loop(0, groups, finish)
+
+    def drain(k):
         scatter(k).wait_send()
         gather(k).wait_send()
-        return 0
-
-    lax.fori_loop(1, chips, drain, 0)
+
+    loop(1, groups, drain)
 
 
 def whole(memory=pltpu.VMEM):
@@ -430,7 +454,7 @@
 def plain(kernel, outs, ins, scratch=(), splits=0, cost=None):
     scratch_shapes = [pltpu.VMEM(shape, jnp.float32) for shape in scratch]
     if splits:
-        scratch_shapes += [pltpu.VMEM((splits, splits), jnp.bfloat16)] * 3
+        scratch_shapes += [pltpu.VMEM((6 * T, splits), jnp.bfloat16)] * 2 + [pltpu.VMEM((splits, splits), jnp.bfloat16)] * 3
     return pl.pallas_call(
         kernel,
         out_shape=tuple(jax.ShapeDtypeStruct(shape, jnp.float32) for shape in outs),
@@ -443,22 +467,19 @@
 
 
 def all_reduce(packed, n):
-    total = packed.shape[0]
-    chips = n // 2
-    half = total // 2
+    groups = n // 4
+    chunk = packed.shape[0] // n
     sems = pltpu.SemaphoreType.DMA
+    pairs = [sems((2 * groups,))] * 2
+    singles = [sems((groups,))] * 2
     return pl.pallas_call(
         functools.partial(reduce_kernel, n),
         out_shape=jax.ShapeDtypeStruct(packed.shape, jnp.float32),
         in_specs=[whole()],
         out_specs=whole(),
-        scratch_shapes=[
-            pltpu.VMEM((half, T), jnp.float32),
-            pltpu.VMEM((half, T), jnp.float32),
-            pltpu.VMEM((chips, half // chips, T), jnp.float32),
-            sems((chips,)), sems((chips,)),
-            sems((chips,)), sems((chips,)), sems((chips,)), sems((chips,)), sems((chips,)), sems((chips,)),
-        ],
+        scratch_shapes=[pltpu.VMEM((2 * groups, chunk, T), jnp.float32)]
+        + [pltpu.VMEM((groups, chunk, T), jnp.float32)] * 4
+        + pairs + singles * 4 + pairs,
         compiler_params=pltpu.CompilerParams(collective_id=0, has_side_effects=True, vmem_limit_bytes=VMEM_LIMIT),
     )(packed)
 

time: 154 us -> 142 us (0.922)
  Pallas kernels: 133 us -> 122 us
    pallas_call x1, Pallas kernels: 33.2 us -> 27.3 us  [body(): plain(functools.partial(second_kernel, cells), [(vectors * nx, ny), squar...]
    pallas_call x1, Pallas kernels: 38.9 us -> 33.2 us  [body(): plain(functools.partial(first_kernel, cells), [square, inner, outer, (tot...]
  transfers between devices with their start and end apart: 2 -> 2, of which waited for: 0 -> 0; matrix products, arithmetic and copies ran while one was open for 2% -> 2% of each run, Pallas kernels for 9% -> 10%
where the time goes in v3:
time: 142 us
  Pallas kernels  122 us (86%)
  local copies, waits for them, and re-layouts  13 us (9%)
  starting transfers between devices  5.45 us (4%)
    pallas_call x2, Pallas kernels, all_reduce(): pl.pallas_call(functools.partial(reduce_kernel, n), out_shape=jax.ShapeDt...  43.3 us
    pallas_call x1, Pallas kernels, body(): plain(functools.partial(first_kernel, cells), [square, inner, outer, (tot...  33.2 us
    pallas_call x1, Pallas kernels, body(): plain(functools.partial(second_kernel, cells), [(vectors * nx, ny), squar...  27.3 us
    pallas_call x1, Pallas kernels, body(): plain(interior_kernel, [inner, (total, T)], 2, [acc], cost=cost)  13.8 us
    ppermute x1, starting transfers between devices, body(): lax.ppermute(edge(0, 0), 'space', [((i + 1) % n, i) for i in range(n)])  4.99 us
    unnamed x10, local copies, waits for them, and re-layouts  4.78 us
    pallas_call x1, Pallas kernels, body(): plain(functools.partial(edge_kernel, nx), [outer, (total, T)], 5, [acc])  4.73 us
    concatenate x2, local copies, waits for them, and re-layouts, edge(): jnp.concatenate([rows, courant_x[b:b + 1], courant_y[b:b + 1], jnp.zeros(...  2.95 us
  transfers between devices with their start and end apart: 2, of which 0 were waited for; matrix products, arithmetic and copies ran while one was open for 2% of the time, Pallas kernels for 10%

profile of v3, /device:TPU:0, one launch (start us, length us, event | category | flops | bytes accessed | tf_op | source)
XLA Modules:
  0.0 141.9 jit_solution(12185822095648214382)
XLA Ops:
  0.6 2.6 %fusion.4 = (f32[512,4,128]{2,1,0:T(4,128)S(1)}, f32[512,4,128]{2,1,0:T(4,128)S(1)}) fusion(f32[512,16,128]{2,1,0:T(8,128)} %param.3), kind=kLoop, calls=%fused_computation.17 | loop fusion | bytes 4194304 | tf_op jit(solution)/shard_map/slice | solution.py:493
  3.2 0.4 maximum_bitcast_fusion
  3.6 0.0 copy-start.3
  3.6 0.0 copy-start.4
  3.7 1.1 fusion.5
  4.8 0.0 copy-done.3
  4.8 0.0 copy-done.4
  4.9 1.5 %concatenate.50 = f32[1032,128]{1,0:T(8,128)} concatenate(f32[1024,128]{1,0:T(8,128)S(1)} %bitcast.27, f32[1,128]{1,0:T(1,128)S(1)} %get-tuple-element.46, f32[1,128]{1,0:T(1,128)S(1)} %get-tuple-element.43, f32[6,128]{1,0:T(8,128)S(1)} %broadcast.65), dimensions={0} | concatenate | bytes 1056768 | tf_op jit(solution)/shard_map/concatenate | solution.py:498
  6.3 0.5 collective-permute-start
  6.8 1.1 copy.9
  7.9 1.5 %concatenate.51 = f32[1032,128]{1,0:T(8,128)} concatenate(f32[1024,128]{1,0:T(8,128)S(1)} %bitcast.28, f32[1,128]{1,0:T(1,128)S(1)} %get-tuple-element.47, f32[1,128]{1,0:T(1,128)S(1)} %get-tuple-element.42, f32[6,128]{1,0:T(8,128)S(1)} %broadcast.65), dimensions={0} | concatenate | bytes 1056768 | tf_op jit(solution)/shard_map/concatenate | solution.py:498
  9.3 5.0 %collective-permute-start.1 = (f32[1032,128]{1,0:T(8,128)}, f32[1032,128]{1,0:T(8,128)S(1)}, u32[]{:S(2)}, u32[]{:S(2)}) collective-permute-start(f32[1032,128]{1,0:T(8,128)} %concatenate.51), channel_id=1, source_target_pairs={{1,0},{2,1},{3,2},{4,3},{5,4},{6,5},{7,6},{8,7},{9,8},{10,9},{11,1... | collective-permute-start | bytes 1585160 | tf_op jit(solution)/shard_map/ppermute | solution.py:505
  14.3 0.4 copy.7
  14.8 13.8 %shard_map.66 = (f32[512,1536]{1,0:T(8,128)S(1)}, f32[1280,128]{1,0:T(8,128)S(1)}) custom-call(f32[8192,128]{1,0:T(8,128)} %bitcast.29, f32[4,16,128]{2,1,0:T(8,128)S(1)} %pad_maximum_fusion.1.coef_ref), custom_call_target="tpu_custom_call" | custom-call | flops 6442450944 | bytes 12582912 | tf_op jit(solution)/shard_map/pallas_call | solution.py:513
  28.6 0.0 copy-start
  28.6 1.7 %copy-done = f32[512,1536]{1,0:T(8,128)} copy-done((f32[512,1536]{1,0:T(8,128)}, f32[512,1536]{1,0:T(8,128)S(1)}, u32[]{:S(2)}) %copy-start) | copy-done | bytes 3145752
  30.3 0.0 collective-permute-done.low_ref
  30.3 0.0 collective-permute-done.1.high_ref
  30.3 4.7 %shard_map.67 = (f32[512,512]{1,0:T(8,128)S(1)}, f32[1280,128]{1,0:T(8,128)S(1)}) custom-call(f32[4096,128]{1,0:T(8,128)S(1)} %bitcast.26, f32[1032,128]{1,0:T(8,128)S(1)} %collective-permute-done.low_ref, f32[1032,128]{1,0:T(8,128)S(1)} %collective-permute-done.1.high_ref, f32[4,18,128]{2,1,0:T(8,128)S(1)} %pad_maximum_fusion.coef_ref, ...), custom_call_target="tpu_custom_call" | custom-call | tf_op jit(solution)/shard_map/pallas_call | solution.py:515
  35.1 20.7 %shard_map.68.packed_ref = f32[1280,128]{1,0:T(8,128)S(1)} custom-call(f32[1280,128]{1,0:T(8,128)S(1)} %get-tuple-element.16.x_ref), custom_call_target="tpu_custom_call" | custom-call | tf_op jit(solution)/shard_map/pallas_call | solution.py:475
  55.8 33.2 %shard_map.69 = (f32[512,512]{1,0:T(8,128)}, f32[512,1536]{1,0:T(8,128)}, f32[512,512]{1,0:T(8,128)S(1)}, f32[1280,128]{1,0:T(8,128)S(1)}) custom-call(f32[1280,128]{1,0:T(8,128)S(1)} %shard_map.68.packed_ref, f32[512,1536]{1,0:T(8,128)} %copy-done, f32[512,512]{1,0:T(8,128)S(1)} %get-tuple-element.18.outer_ref), custom_call_target="tpu_custom_call" | custom-call | tf_op jit(solution)/shard_map/pallas_call | solution.py:520
  89.0 22.5 %shard_map.70.packed_ref = f32[1280,128]{1,0:T(8,128)S(1)} custom-call(f32[1280,128]{1,0:T(8,128)S(1)} %get-tuple-element.19.x_ref), custom_call_target="tpu_custom_call" | custom-call | tf_op jit(solution)/shard_map/pallas_call | solution.py:475
  111.5 0.0 copy-start.1
  111.5 1.9 %copy-done.1 = f32[512,1536]{1,0:T(8,128)S(1)} copy-done((f32[512,1536]{1,0:T(8,128)S(1)}, f32[512,1536]{1,0:T(8,128)}, u32[]{:S(2)}) %copy-start.1) | copy-done | bytes 3145752
  113.4 0.0 copy-start.2
  113.4 1.2 copy-done.2
  114.6 27.3 %shard_map.71 = (f32[8192,128]{1,0:T(8,128)}, f32[512,512]{1,0:T(8,128)}, f32[4,128]{1,0:T(4,128)}) custom-call(f32[1280,128]{1,0:T(8,128)S(1)} %shard_map.70.packed_ref, f32[512,1536]{1,0:T(8,128)S(1)} %copy-done.1, f32[512,512]{1,0:T(8,128)S(1)} %get-tuple-element.21.outer_ref, f32[512,512]{1,0:T(8,128)S(1)} %copy-done.2), custom_call_target="tpu_custom_call" | custom-call | tf_op jit(solution)/shard_map/pallas_call | solution.py:524
  (10 shorter events, 0.1 us)
Async XLA Ops:
  3.6 1.2 copy-start.3
  3.6 1.2 copy-start.4
  6.3 23.9 %collective-permute-start = (f32[1032,128]{1,0:T(8,128)}, f32[1032,128]{1,0:T(8,128)S(1)}, u32[]{:S(2)}, u32[]{:S(2)}) collective-permute-start(f32[1032,128]{1,0:T(8,128)} %concatenate.50), channel_id=1, source_target_pairs={{0,1},{1,2},{2,3},{3,4},{4,5},{5,6},{6,7},{7,8},{8,9},{9,10},{10,1... | collective-permute-start | bytes 1585160 | tf_op jit(solution)/shard_map/ppermute | solution.py:504
  9.3 20.9 %collective-permute-start.1 = (f32[1032,128]{1,0:T(8,128)}, f32[1032,128]{1,0:T(8,128)S(1)}, u32[]{:S(2)}, u32[]{:S(2)}) collective-permute-start(f32[1032,128]{1,0:T(8,128)} %concatenate.51), channel_id=1, source_target_pairs={{1,0},{2,1},{3,2},{4,3},{5,4},{6,5},{7,6},{8,7},{9,8},{10,9},{11,1... | collective-permute-start | bytes 1585160 | tf_op jit(solution)/shard_map/ppermute | solution.py:505
  28.6 1.7 %copy-start = (f32[512,1536]{1,0:T(8,128)}, f32[512,1536]{1,0:T(8,128)S(1)}, u32[]{:S(2)}) copy-start(f32[512,1536]{1,0:T(8,128)S(1)} %get-tuple-element.17.inner_ref) | copy-start | bytes 9437188
  111.5 1.9 %copy-start.1 = (f32[512,1536]{1,0:T(8,128)S(1)}, f32[512,1536]{1,0:T(8,128)}, u32[]{:S(2)}) copy-start(f32[512,1536]{1,0:T(8,128)} %get-tuple-element.20.inner_ref) | copy-start | bytes 9437188
  113.4 1.2 copy-start.2

commit v4 on v3

--- a/solution.py
+++ b/solution.py
@@ -151,6 +151,22 @@
         one.append(apply(*zero[-3:], coef_ref, coef_at(x)))
         if len(one) >= 3:
             store(x - 1, apply(*one[-3:], coef_ref, coef_at(x - 1)))
+
+
+def pick_kernel(w_ref, cx_ref, cy_ref, mine_ref, low_ref, high_ref):
+    nx = cx_ref.shape[0]
+    vectors = w_ref.shape[0] // nx
+    for at in range(8):
+        x = at if at < 4 else nx - 8 + at
+        value = w_ref[pl.ds(x, vectors, stride=nx), :]
+        mine_ref[at * vectors:(at + 1) * vectors, :] = value
+        if at < 2:
+            high_ref[at * vectors:(at + 1) * vectors, :] = value
+        if at >= 6:
+            low_ref[(at - 6) * vectors:(at - 5) * vectors, :] = value
+    zeros = jnp.zeros((6, T), jnp.float32)
+    for ref, x in ((low_ref, nx - 1), (high_ref, 0)):
+        ref[2 * vectors:, :] = jnp.concatenate([cx_ref[x:x + 1, :], cy_ref[x:x + 1, :], zeros], axis=0)
 
 
 def interior_kernel(w_ref, coef_ref, v_ref, packed_ref, acc_ref):
@@ -490,19 +506,16 @@
     width = nx * ny
     cells = float(width * n)
 
-    pick = jnp.concatenate([tangent[:, :4], tangent[:, nx - 4:]], axis=1)
-    mine = jnp.transpose(pick, (1, 0, 2)).reshape(8 * vectors, ny)
-
-    def edge(a, b):
-        rows = mine[a * vectors:(a + 2) * vectors]
-        return jnp.concatenate([rows, courant_x[b:b + 1], courant_y[b:b + 1], jnp.zeros((6, ny), jnp.float32)], axis=0)
+    flat = tangent.reshape(vectors * nx, ny)
+    sent = (2 * vectors + 8, ny)
+    mine, low, high = plain(pick_kernel, [(8 * vectors, ny), sent, sent], 3)(flat, courant_x, courant_y)
 
     def coefficients(x, y):
         x, y = 0.5 * x, 0.5 * y
         return jnp.stack([diffusion_number - x, diffusion_number + x, diffusion_number - y, diffusion_number + y])
 
-    low = lax.ppermute(edge(6, nx - 1), "space", [(i, (i + 1) % n) for i in range(n)])
-    high = lax.ppermute(edge(0, 0), "space", [((i + 1) % n, i) for i in range(n)])
+    low = lax.ppermute(low, "space", [(i, (i + 1) % n) for i in range(n)])
+    high = lax.ppermute(high, "space", [((i + 1) % n, i) for i in range(n)])
     e = 2 * vectors
     cx = jnp.concatenate([low[e:e + 1], courant_x, high[e:e + 1]], axis=0)
     cy = jnp.concatenate([low[e + 1:e + 2], courant_y, high[e + 1:e + 2]], axis=0)
@@ -511,7 +524,7 @@
     acc = gram_scratch(vectors)
     cost = pl.CostEstimate(flops=12 * vectors * vectors * width, bytes_accessed=12 * vectors * width, transcendentals=0)
     v_inner, part = plain(interior_kernel, [inner, (total, T)], 2, [acc], cost=cost)(
-        tangent.reshape(vectors * nx, ny), coefficients(courant_x, courant_y))
+        flat, coefficients(courant_x, courant_y))
     v_outer, packed = plain(functools.partial(edge_kernel, nx), [outer, (total, T)], 5, [acc])(
         mine, low, high, coefficients(cx, cy), part)
     packed = all_reduce(packed, n)

time: 142 us -> 138 us (0.972)
  local copies, waits for them, and re-layouts: 13 us -> 6.17 us
  Pallas kernels: 122 us -> 125 us
    slice x5 -> x0, local copies, waits for them, and re-layouts: 4.81 us -> none  [the longest x1 2.59 us: body(): pick = jnp.concatenate([tangent[:, :4], tangent[:, nx - 4:]], axis=1)]
    pallas_call x0 -> x1, Pallas kernels: none -> 3.18 us  [body(): plain(pick_kernel, [(8 * vectors, ny), sent, sent], 3)]
    concatenate x2 -> x0, local copies, waits for them, and re-layouts: 2.95 us -> none  [edge(): jnp.concatenate([rows, courant_x[b:b + 1], courant_y[b:b + 1], jnp.zeros(...]
    unnamed x10 -> x14, local copies, waits for them, and re-layouts: 4.78 us -> 6.17 us
  transfers between devices with their start and end apart: 2 -> 2, of which waited for: 0 -> 0; matrix products, arithmetic and copies ran while one was open for 2% -> 0% of each run, Pallas kernels for 10% -> 10%
where the time goes in v4:
time: 138 us
  Pallas kernels  125 us (91%)
  local copies, waits for them, and re-layouts  6.17 us (4%)
  starting transfers between devices  5.56 us (4%)
    pallas_call x2, Pallas kernels, all_reduce(): pl.pallas_call(functools.partial(reduce_kernel, n), out_shape=jax.ShapeDt...  43.3 us
    pallas_call x1, Pallas kernels, body(): plain(functools.partial(first_kernel, cells), [square, inner, outer, (tot...  33.2 us
    pallas_call x1, Pallas kernels, body(): plain(functools.partial(second_kernel, cells), [(vectors * nx, ny), squar...  27.2 us
    pallas_call x1, Pallas kernels, body(): plain(interior_kernel, [inner, (total, T)], 2, [acc], cost=cost)  13.8 us
    unnamed x14, local copies, waits for them, and re-layouts  6.17 us
    ppermute x1, starting transfers between devices, body(): high = lax.ppermute(high, 'space', [((i + 1) % n, i) for i in range(n)])  5.06 us
    pallas_call x1, Pallas kernels, body(): plain(functools.partial(edge_kernel, nx), [outer, (total, T)], 5, [acc])  4.74 us
    pallas_call x1, Pallas kernels, body(): plain(pick_kernel, [(8 * vectors, ny), sent, sent], 3)  3.18 us
  transfers between devices with their start and end apart: 2, of which 0 were waited for; matrix products, arithmetic and copies ran while one was open for 0% of the time, Pallas kernels for 10%

profile of v4, /device:TPU:0, one launch (start us, length us, event | category | flops | bytes accessed | tf_op | source)
XLA Modules:
  0.0 137.9 jit_solution(968339223051886330)
XLA Ops:
  0.6 0.0 copy-start.3
  0.6 0.7 copy-done.3
  1.3 0.0 copy-start.5
  1.3 0.7 copy-done.5
  2.0 3.2 %shard_map.66 = (f32[4096,128]{1,0:T(8,128)S(1)}, f32[1032,128]{1,0:T(8,128)S(1)}, f32[1032,128]{1,0:T(8,128)S(1)}) custom-call(f32[8192,128]{1,0:T(8,128)} %bitcast.23, f32[16,128]{1,0:T(8,128)S(1)} %copy-done.3, f32[16,128]{1,0:T(8,128)S(1)} %copy-done.5), custom_call_target="tpu_custom_call" | custom-call | tf_op jit(solution)/shard_map/pallas_call | solution.py:511
  5.2 0.5 collective-permute-start
  5.7 5.1 %collective-permute-start.1 = (f32[1032,128]{1,0:T(8,128)S(1)}, f32[1032,128]{1,0:T(8,128)S(1)}, u32[]{:S(2)}, u32[]{:S(2)}) collective-permute-start(f32[1032,128]{1,0:T(8,128)S(1)} %get-tuple-element.20), channel_id=1, source_target_pairs={{1,0},{2,1},{3,2},{4,3},{5,4},{6,5},{7,6},{8,7},{9,8},{10,9},{11,1... | collective-permute-start | bytes 1585160 | tf_op jit(solution)/shard_map/ppermute | solution.py:518
  10.8 0.0 copy-start.4
  10.8 0.0 copy-start.6
  10.8 13.8 %shard_map.67 = (f32[512,1536]{1,0:T(8,128)S(1)}, f32[1280,128]{1,0:T(8,128)S(1)}) custom-call(f32[8192,128]{1,0:T(8,128)} %bitcast.24, f32[4,16,128]{2,1,0:T(8,128)S(1)} %pad_maximum_fusion.1.coef_ref), custom_call_target="tpu_custom_call" | custom-call | flops 6442450944 | bytes 12582912 | tf_op jit(solution)/shard_map/pallas_call | solution.py:526
  24.6 0.0 copy-start
  24.6 1.7 %copy-done = f32[512,1536]{1,0:T(8,128)} copy-done((f32[512,1536]{1,0:T(8,128)}, f32[512,1536]{1,0:T(8,128)S(1)}, u32[]{:S(2)}) %copy-start) | copy-done | bytes 3145752
  26.3 0.0 collective-permute-done.low_ref
  26.3 0.0 collective-permute-done.1.high_ref
  26.3 0.0 copy-done.4
  26.3 0.0 copy-done.6
  26.4 4.7 %shard_map.68 = (f32[512,512]{1,0:T(8,128)S(1)}, f32[1280,128]{1,0:T(8,128)S(1)}) custom-call(f32[4096,128]{1,0:T(8,128)S(1)} %get-tuple-element.18.mine_ref, f32[1032,128]{1,0:T(8,128)S(1)} %collective-permute-done.low_ref, f32[1032,128]{1,0:T(8,128)S(1)} %collective-permute-done.1.high_ref, f32[4,18,128]{2,1,0:T(8,128)S(1)} %pad_maximum_fusion.coef_ref, ...), custom_call_target="tpu_custom_call" | custom-call | tf_op jit(solution)/shard_map/pallas_call | solution.py:528
  31.1 20.7 %shard_map.69.packed_ref = f32[1280,128]{1,0:T(8,128)S(1)} custom-call(f32[1280,128]{1,0:T(8,128)S(1)} %get-tuple-element.22.x_ref), custom_call_target="tpu_custom_call" | custom-call | tf_op jit(solution)/shard_map/pallas_call | solution.py:491
  51.8 33.2 %shard_map.70 = (f32[512,512]{1,0:T(8,128)}, f32[512,1536]{1,0:T(8,128)}, f32[512,512]{1,0:T(8,128)S(1)}, f32[1280,128]{1,0:T(8,128)S(1)}) custom-call(f32[1280,128]{1,0:T(8,128)S(1)} %shard_map.69.packed_ref, f32[512,1536]{1,0:T(8,128)} %copy-done, f32[512,512]{1,0:T(8,128)S(1)} %get-tuple-element.24.outer_ref), custom_call_target="tpu_custom_call" | custom-call | tf_op jit(solution)/shard_map/pallas_call | solution.py:533
  85.0 22.6 %shard_map.71.packed_ref = f32[1280,128]{1,0:T(8,128)S(1)} custom-call(f32[1280,128]{1,0:T(8,128)S(1)} %get-tuple-element.25.x_ref), custom_call_target="tpu_custom_call" | custom-call | tf_op jit(solution)/shard_map/pallas_call | solution.py:491
  107.6 0.0 copy-start.1
  107.6 1.9 %copy-done.1 = f32[512,1536]{1,0:T(8,128)S(1)} copy-done((f32[512,1536]{1,0:T(8,128)S(1)}, f32[512,1536]{1,0:T(8,128)}, u32[]{:S(2)}) %copy-start.1) | copy-done | bytes 3145752
  109.5 0.0 copy-start.2
  109.5 1.2 copy-done.2
  110.7 27.2 %shard_map.72 = (f32[8192,128]{1,0:T(8,128)}, f32[512,512]{1,0:T(8,128)}, f32[4,128]{1,0:T(4,128)}) custom-call(f32[1280,128]{1,0:T(8,128)S(1)} %shard_map.71.packed_ref, f32[512,1536]{1,0:T(8,128)S(1)} %copy-done.1, f32[512,512]{1,0:T(8,128)S(1)} %get-tuple-element.27.outer_ref, f32[512,512]{1,0:T(8,128)S(1)} %copy-done.2), custom_call_target="tpu_custom_call" | custom-call | tf_op jit(solution)/shard_map/pallas_call | solution.py:537
  (6 shorter events, 0.0 us)
Async XLA Ops:
  0.6 0.7 copy-start.3
  1.3 0.7 copy-start.5
  5.2 21.1 %collective-permute-start = (f32[1032,128]{1,0:T(8,128)S(1)}, f32[1032,128]{1,0:T(8,128)S(1)}, u32[]{:S(2)}, u32[]{:S(2)}) collective-permute-start(f32[1032,128]{1,0:T(8,128)S(1)} %get-tuple-element.19), channel_id=1, source_target_pairs={{0,1},{1,2},{2,3},{3,4},{4,5},{5,6},{6,7},{7,8},{8,9},{9,10},{10,1... | collective-permute-start | bytes 1585160 | tf_op jit(solution)/shard_map/ppermute | solution.py:517
  5.7 20.6 %collective-permute-start.1 = (f32[1032,128]{1,0:T(8,128)S(1)}, f32[1032,128]{1,0:T(8,128)S(1)}, u32[]{:S(2)}, u32[]{:S(2)}) collective-permute-start(f32[1032,128]{1,0:T(8,128)S(1)} %get-tuple-element.20), channel_id=1, source_target_pairs={{1,0},{2,1},{3,2},{4,3},{5,4},{6,5},{7,6},{8,7},{9,8},{10,9},{11,1... | collective-permute-start | bytes 1585160 | tf_op jit(solution)/shard_map/ppermute | solution.py:518
  10.8 15.5 %copy-start.4 = (f32[16,128]{1,0:T(8,128)S(1)}, f32[16,128]{1,0:T(8,128)}, u32[]{:S(2)}) copy-start(f32[16,128]{1,0:T(8,128)} %cx_ref.1) | copy-start | bytes 24580
  10.8 15.5 %copy-start.6 = (f32[16,128]{1,0:T(8,128)S(1)}, f32[16,128]{1,0:T(8,128)}, u32[]{:S(2)}) copy-start(f32[16,128]{1,0:T(8,128)} %cy_ref.1) | copy-start | bytes 24580
  24.6 1.7 %copy-start = (f32[512,1536]{1,0:T(8,128)}, f32[512,1536]{1,0:T(8,128)S(1)}, u32[]{:S(2)}) copy-start(f32[512,1536]{1,0:T(8,128)S(1)} %get-tuple-element.23.inner_ref) | copy-start | bytes 9437188
  107.6 1.9 %copy-start.1 = (f32[512,1536]{1,0:T(8,128)S(1)}, f32[512,1536]{1,0:T(8,128)}, u32[]{:S(2)}) copy-start(f32[512,1536]{1,0:T(8,128)} %get-tuple-element.26.inner_ref) | copy-start | bytes 9437188
  109.5 1.2 copy-start.2
